TPU v7x, 32 devices: a whole 2x2x4 slice. The times are simulated.
32 devices in a mesh: wide: 16 (over z, y, x), narrow: 2 (over core).
Axes of the slice: x: 2, y: 2, z: 4, core: 2. Of those that a mesh axis runs over, the one named last changes fastest.
Arguments:
- point_feats: bfloat16 [8192, 512], P(('wide', 'narrow')), may hold values from -24 to 24
- region_ids: int32 [2048], P(('wide', 'narrow')), may hold values from 0 to 63, as said below
- w_qkv: bfloat16 [512, 1536], replicated, may hold values from -0.25 to 0.25
- w_out: bfloat16 [512, 512], replicated, may hold values from -0.25 to 0.25
- w_expert_in: bfloat16 [512, 131072], P(None, 'wide'), may hold values from -0.25 to 0.25
- b_expert_in: float32 [131072], P('wide'), may hold values from -4 to 4
- w_expert_out: bfloat16 [131072, 512], P('wide'), may hold values from -0.125 to 0.125
- out_cotangent: bfloat16 [8192, 512], P(('wide', 'narrow')), may hold values from -18 to 18
Outputs:
- layer_out: bfloat16 [8192, 512], P(('wide', 'narrow'))
- grad_feats: bfloat16 [8192, 512], P(('wide', 'narrow'))
- grad_attention: float32 [512, 2048], P(('wide', 'narrow'))
- grad_expert_in: float32 [512, 131072], P('narrow', 'wide')
- grad_expert_out: float32 [131072, 512], P('wide', 'narrow')
- grad_expert_bias: float32 [131072], P(('wide', 'narrow'))
Inputs may be any that keep to these rules, and one draw needn't show every extreme that they name: `region_ids`: the 64 blocks of one device name any one region at most 2 times, and one region is named exactly 2 times by the blocks of every device.
All inputs are finite; a program needn't handle non-finite values.
Results may differ from a plain program's by a relative error of at most 0.0095.
Values may be sent and summed in bfloat16 or wider, within the bound.
A program may use at most 128 MiB of HBM per device.

v0:
```python
import jax
import jax.numpy as jnp
from jax import lax
from jax.sharding import PartitionSpec as P

HEADS = 8
HID = 2048
DOMAIN_SPECIALS = 64
DOMAIN_REPEAT_CAP = 2


gelu_scale = 0.7978845608
gelu_cubic = 0.044715


def gelu_value(values):
    inner = gelu_scale * (values + gelu_cubic * values * values * values)
    return 0.5 * values * (1.0 + jnp.tanh(inner))


def gelu_slope(values):
    tangent = jnp.tanh(gelu_scale * (values + gelu_cubic * values * values * values))
    return 0.5 * (1.0 + tangent) + 0.5 * values * (1.0 - tangent * tangent) * gelu_scale * (
        1.0 + 3.0 * gelu_cubic * values * values
    )


def normalize_heads(raw):
    floats = raw.astype(jnp.float32)
    centred = floats - jnp.mean(floats, axis=-1, keepdims=True)
    scale_dev = jnp.sqrt(jnp.mean(centred * centred, axis=-1, keepdims=True) + 1e-05)
    normed = centred / scale_dev
    return (normed.astype(jnp.bfloat16), normed, scale_dev)


def normalize_back(grad_normed, normed, scale_dev):
    mean_grad = jnp.mean(grad_normed, axis=-1, keepdims=True)
    mean_cross = jnp.mean(grad_normed * normed, axis=-1, keepdims=True)
    return (grad_normed - mean_grad - normed * mean_cross) / scale_dev


def on_device(
    point_feats, region_ids, w_qkv, w_out, w_expert_in, b_expert_in, w_expert_out, out_cotangent
):
    wide_count = lax.axis_size("wide")
    narrow_count = lax.axis_size("narrow")
    points_local, width = point_feats.shape
    total_points = points_local * wide_count * narrow_count
    head_dim = width // HEADS
    qkv = jnp.dot(point_feats, w_qkv, preferred_element_type=jnp.float32).astype(jnp.bfloat16)
    queries = qkv[:, :width].reshape(points_local, HEADS, head_dim)
    key_norm, key_unit, key_scale = normalize_heads(
        qkv[:, width : 2 * width].reshape(points_local, HEADS, head_dim)
    )
    value_norm, value_unit, value_scale = normalize_heads(
        qkv[:, 2 * width :].reshape(points_local, HEADS, head_dim)
    )
    grad_mixed = jnp.einsum(
        "pc,ic->pi", out_cotangent, w_out, preferred_element_type=jnp.float32
    ).astype(jnp.bfloat16)
    grad_heads = grad_mixed.reshape(points_local, HEADS, head_dim)
    local_summary = jnp.einsum(
        "phi,phj->hij", key_norm, value_norm, preferred_element_type=jnp.float32
    )
    local_grad = jnp.einsum("phi,phj->hij", queries, grad_heads, preferred_element_type=jnp.float32)
    summary_total, grad_total = lax.psum((local_summary, local_grad), ("wide", "narrow"))
    summary_b = (summary_total / total_points).astype(jnp.bfloat16)
    grad_summary = grad_total / total_points
    mixed = (
        jnp.einsum("phi,hij->phj", queries, summary_b, preferred_element_type=jnp.float32)
        .astype(jnp.bfloat16)
        .reshape(points_local, width)
    )
    attention = jnp.dot(mixed, w_out, preferred_element_type=jnp.float32)
    grad_query = jnp.einsum(
        "phj,hij->phi", grad_heads, summary_b, preferred_element_type=jnp.float32
    ).astype(jnp.bfloat16)
    grad_keynorm = jnp.einsum("phj,hij->phi", value_norm.astype(jnp.float32), grad_summary)
    grad_valnorm = jnp.einsum("phi,hij->phj", key_norm.astype(jnp.float32), grad_summary)
    grad_key = normalize_back(grad_keynorm, key_unit, key_scale).astype(jnp.bfloat16)
    grad_value = normalize_back(grad_valnorm, value_unit, value_scale).astype(jnp.bfloat16)
    grad_qkv = jnp.concatenate(
        [
            grad_query.reshape(points_local, width),
            grad_key.reshape(points_local, width),
            grad_value.reshape(points_local, width),
        ],
        axis=1,
    )
    attention_back = jnp.einsum("pc,ic->pi", grad_qkv, w_qkv, preferred_element_type=jnp.float32)
    first_part = jnp.einsum("pi,pc->ic", point_feats, grad_qkv, preferred_element_type=jnp.float32)
    second_part = jnp.einsum("pi,pc->ic", mixed, out_cotangent, preferred_element_type=jnp.float32)
    grad_attention = lax.psum_scatter(
        jnp.concatenate([first_part, second_part], axis=1) / total_points,
        ("wide", "narrow"),
        scatter_dimension=0,
        tiled=True,
    )
    slab_cols = w_expert_in.shape[1]
    owner_count = max(1, wide_count // DOMAIN_SPECIALS)
    experts_here = max(1, DOMAIN_SPECIALS // wide_count)
    slot_cap = DOMAIN_REPEAT_CAP * experts_here
    blocks_local = region_ids.shape[0]
    block_len = points_local // blocks_local
    slot_total = wide_count * slot_cap
    dest_group = region_ids // experts_here
    same_group = dest_group[:, None] == dest_group[None, :]
    earlier = lax.broadcasted_iota(
        jnp.int32, (blocks_local, blocks_local), 1
    ) < lax.broadcasted_iota(jnp.int32, (blocks_local, blocks_local), 0)
    block_rank = jnp.sum((same_group & earlier).astype(jnp.int32), axis=1)
    first_dest = dest_group * owner_count
    slot_ids = jnp.arange(slot_total, dtype=jnp.int32)
    slot_dest = slot_ids // slot_cap
    slot_pos = slot_ids % slot_cap
    matches = (
        (slot_dest[:, None] >= first_dest[None, :])
        & (slot_dest[:, None] < first_dest[None, :] + owner_count)
        & (slot_pos[:, None] == block_rank[None, :])
    )
    filled = jnp.any(matches, axis=1)
    source_block = jnp.sum(
        jnp.where(matches, jnp.arange(blocks_local, dtype=jnp.int32)[None, :], 0), axis=1
    )
    send_labels = jnp.where(filled, region_ids[source_block], -1)

    def pack_rows(data):
        rows = jnp.take(data.reshape(blocks_local, block_len * width), source_block, axis=0)
        rows = jnp.where(filled[:, None], rows, jnp.zeros_like(rows))
        return rows.reshape(slot_total * block_len, width)

    col_expert = (
        lax.axis_index("wide") * slab_cols + jnp.arange(slab_cols, dtype=jnp.int32)
    ) // HID
    recv_feats, recv_labels = (
        lax.all_to_all(pack_rows(point_feats), "wide", split_axis=0, concat_axis=0, tiled=True),
        lax.all_to_all(send_labels, "wide", split_axis=0, concat_axis=0, tiled=True),
    )
    row_labels = jnp.repeat(recv_labels, block_len)
    live_mask = row_labels[:, None] == col_expert[None, :]
    pre_act = jnp.dot(recv_feats, w_expert_in, preferred_element_type=jnp.float32) + b_expert_in
    hidden = jnp.where(live_mask, gelu_value(pre_act), 0.0).astype(jnp.bfloat16)
    partial_out = jnp.dot(hidden, w_expert_out, preferred_element_type=jnp.float32).astype(
        jnp.bfloat16
    )
    live_mask, pre_act, hidden, partial_out = (live_mask, pre_act, hidden, partial_out)
    returned_out = lax.all_to_all(partial_out, "wide", split_axis=0, concat_axis=0, tiled=True)
    recv_cots = lax.all_to_all(
        pack_rows(out_cotangent), "wide", split_axis=0, concat_axis=0, tiled=True
    )
    grad_hidden = jnp.einsum(
        "rd,sd->rs", recv_cots, w_expert_out, preferred_element_type=jnp.float32
    )
    grad_pre = jnp.where(live_mask, grad_hidden * gelu_slope(pre_act), 0.0).astype(jnp.bfloat16)
    grad_second = jnp.einsum("rs,rd->sd", hidden, recv_cots, preferred_element_type=jnp.float32)
    grad_first = jnp.einsum("rd,rs->ds", recv_feats, grad_pre, preferred_element_type=jnp.float32)
    grad_bias = jnp.sum(grad_pre.astype(jnp.float32), axis=0)
    partial_back = jnp.einsum(
        "rs,ds->rd", grad_pre, w_expert_in, preferred_element_type=jnp.float32
    ).astype(jnp.bfloat16)
    grad_first, grad_second, grad_bias, partial_back = (
        grad_first,
        grad_second,
        grad_bias,
        partial_back,
    )
    returned_back = lax.all_to_all(partial_back, "wide", split_axis=0, concat_axis=0, tiled=True)
    pick_rows = (
        first_dest[:, None] + jnp.arange(owner_count, dtype=jnp.int32)[None, :]
    ) * slot_cap + block_rank[:, None]

    def unpack_rows(returned):
        rows = jnp.take(returned.reshape(slot_total, block_len * width), pick_rows, axis=0)
        return jnp.sum(rows.astype(jnp.float32), axis=1).reshape(points_local, width)

    layer_out = (point_feats.astype(jnp.float32) + attention + unpack_rows(returned_out)).astype(
        jnp.bfloat16
    )
    grad_feats = (
        out_cotangent.astype(jnp.float32) + attention_back + unpack_rows(returned_back)
    ).astype(jnp.bfloat16)
    share = DOMAIN_SPECIALS / total_points
    grad_first = grad_first * share
    grad_second = grad_second * share
    grad_bias = grad_bias * share
    grad_in, grad_out_w, grad_bias_out = (
        lax.psum_scatter(
            grad_first.astype(jnp.bfloat16), "narrow", scatter_dimension=0, tiled=True
        ).astype(jnp.float32),
        lax.psum_scatter(
            grad_second.astype(jnp.bfloat16), "narrow", scatter_dimension=1, tiled=True
        ).astype(jnp.float32),
        lax.psum_scatter(
            grad_bias.astype(jnp.bfloat16), "narrow", scatter_dimension=0, tiled=True
        ).astype(jnp.float32),
    )
    return (layer_out, grad_feats, grad_attention, grad_in, grad_out_w, grad_bias_out)


def solution(mesh):
    placed = (
        P(("wide", "narrow"), None),
        P(("wide", "narrow")),
        P(),
        P(),
        P(None, "wide"),
        P("wide"),
        P("wide", None),
        P(("wide", "narrow"), None),
    )
    return jax.shard_map(
        on_device,
        mesh=mesh,
        in_specs=placed,
        out_specs=(
            P(("wide", "narrow"), None),
            P(("wide", "narrow"), None),
            P(("wide", "narrow"), None),
            P("narrow", "wide"),
            P("wide", "narrow"),
            P(("wide", "narrow")),
        ),
        check_vma=False,
    )
```

profile of v0, /device:TPU:0, one launch (start us, length us, event | category | flops | bytes accessed | tf_op | source)
XLA Modules:
  0.0 344.9 jit_solution(8937103089254830047)
XLA Ops:
  9.3 1.6 gather_fusion
  11.5 8.3 %all-to-all-start = ((s32[16,8,1]{1,2,0:T(1,128)}), s32[16,8,1]{1,2,0:T(1,128)S(1)}, u32[]{:S(2)}, u32[]{:S(2)}) async-start(s32[16,8,1]{1,2,0:T(1,128)} %bitcast.9), calls=%async_computation | async-start | bytes 16384 | tf_op jit(solution)/shard_map/all_to_all | solution.py:137
  19.9 1.1 reshape.259
  21.0 1.1 reshape.251
  22.2 1.7 gather_fusion.3
  23.9 1.7 gather_fusion.1
  26.2 1.1 slice_convert_fusion
  27.3 1.2 copy.39
  28.6 1.2 copy.38
  29.9 2.1 convolution_convert_fusion.4
  32.0 2.2 select_select_fusion
  34.2 1.1 all_to_all.36
  35.3 7.0 %all-to-all-start.1 = ((bf16[16,32,512]{2,1,0:T(8,128)(2,1)}), bf16[16,32,512]{2,1,0:T(8,128)(2,1)}, u32[]{:S(2)}, u32[]{:S(2)}) async-start(bf16[16,32,512]{2,1,0:T(8,128)(2,1)} %all_to_all.36), calls=%async_computation.1 | async-start | bytes 1048576 | tf_op jit(solution)/shard_map/all_to_all | solution.py:136
  42.4 1.1 copy.40
  43.5 1.1 copy.43
  44.7 0.9 fusion.42
  45.6 0.9 fusion.35
  46.6 2.2 all_to_all.41
  50.3 6.7 %all-to-all-done.1 = bf16[16,32,512]{2,1,0:T(8,128)(2,1)} async-done(((bf16[16,32,512]{2,1,0:T(8,128)(2,1)}), bf16[16,32,512]{2,1,0:T(8,128)(2,1)}, u32[]{:S(2)}, u32[]{:S(2)}) %all-to-all-start.1) | async-done | bytes 524320 | tf_op jit(solution)/shard_map/all_to_all | solution.py:136
  56.9 4.2 %all-to-all-start.3 = ((bf16[16,32,512]{2,1,0:T(8,128)(2,1)}), bf16[16,32,512]{2,1,0:T(8,128)(2,1)}, u32[]{:S(2)}, u32[]{:S(2)}) async-start(bf16[16,32,512]{2,1,0:T(8,128)(2,1)} %all_to_all.41), calls=%async_computation.3 | async-start | bytes 1048576 | tf_op jit(solution)/shard_map/all_to_all | solution.py:148
  61.4 16.2 %fusion = (bf16[512,8192]{1,0:T(8,128)(2,1)}, f32[512,8192]{1,0:T(8,128)}) fusion(f32[8192]{0:T(1024)} %param.17, s32[8192]{0:T(1024)S(1)} %add_select_fusion, s32[512]{0:T(512)S(1)} %eq.49, bf16[512,512]{1,0:T(8,128)(2,1)} %bitcast.10, bf16[512,8192]{1,0:T(8,128)(2,1)} %param.16), kind=kOutput, calls=%fused_computation.9 | convolution fusion | flops 4345298944 | bytes 34146304 | tf_op jit(solution)/shard_map/dot_general | solution.py:141
  77.6 23.2 %convert_reduce_fusion = (f32[8192]{0:T(1024)S(1)}, bf16[512,8192]{1,0:T(8,128)(2,1)}) fusion(f32[512,8192]{1,0:T(8,128)} %get-tuple-element.48, f32[8192]{0:T(1024)} %param.17, bf16[512,512]{1,0:T(8,128)(2,1)} %bitcast.22, bf16[8192,512]{1,0:T(8,128)(2,1)} %param.18, s32[8192]{0:T(1024)S(1)} %add_select_fusion, s32[512]{0:T(512)S(1)} %eq.49), kind=kOutput, calls=%fused_computation.17 | convolution fusion | flops 4395622400 | bytes 34179072 | tf_op jit(solution)/shard_map/rd,sd->rs/dot_general | solution.py:151
  100.8 11.4 %multiply_convert_fusion.1 = bf16[512,8192]{1,0:T(8,128)(2,1)} fusion(bf16[512,512]{1,0:T(8,128)(2,1)} %bitcast.10, bf16[512,8192]{1,0:T(8,128)(2,1)} %get-tuple-element.52), kind=kOutput, calls=%fused_computation.19 | convolution fusion | flops 4303355904 | bytes 17301504 | tf_op jit(solution)/shard_map/rd,rs->ds/dot_general | solution.py:156
  112.2 12.7 %multiply_convert_fusion = bf16[8192,512]{1,0:T(8,128)(2,1)} fusion(bf16[512,8192]{1,0:T(8,128)(2,1)} %get-tuple-element.47, bf16[512,512]{1,0:T(8,128)(2,1)} %bitcast.22), kind=kOutput, calls=%fused_computation.18 | convolution fusion | flops 4303355904 | bytes 17301504 | tf_op jit(solution)/shard_map/rs,rd->sd/dot_general | solution.py:155
  125.0 57.1 %all-reduce.4.cloned.1.call-done = (f32[8,64,64]{2,1,0:T(8,128)}, f32[8,64,64]{2,1,0:T(8,128)}) async-done(((f32[8,64,64]{2,1,0:T(8,128)}, f32[8,64,64]{2,1,0:T(8,128)}), (f32[8,64,64]{2,1,0:T(8,128)}, f32[8,64,64]{2,1,0:T(8,128)})) %all-reduce.4.cloned.1.call-update) | async-done | bytes 262160 | tf_op jit(solution)/shard_map/psum | solution.py:66
  182.1 1.3 fusion.41
  183.4 1.2 fusion.40
  186.7 2.4 maximum_multiply_fusion
  189.2 5.7 %copy.48 = f32[512,2048]{1,0:T(8,128)} copy(f32[512,2048]{0,1:T(8,128)} %maximum_multiply_fusion) | data formatting | bytes 8388608
  194.9 11.2 %convolution_convert_fusion.1 = bf16[512,512]{1,0:T(8,128)(2,1)} fusion(bf16[512,8192]{1,0:T(8,128)(2,1)} %get-tuple-element.52, bf16[512,8192]{1,0:T(8,128)(2,1)} %param.16), kind=kOutput, calls=%fused_computation.23 | convolution fusion | flops 4295229440 | bytes 17301504 | tf_op jit(solution)/shard_map/rs,ds->rd/dot_general | solution.py:158
  206.1 4.5 %all-to-all-start.4 = ((bf16[16,32,512]{2,1,0:T(8,128)(2,1)}), bf16[16,32,512]{2,1,0:T(8,128)(2,1)S(1)}, u32[]{:S(2)}, u32[]{:S(2)}) async-start(bf16[16,32,512]{2,1,0:T(8,128)(2,1)} %bitcast.23), calls=%async_computation.4 | async-start | bytes 1048576 | tf_op jit(solution)/shard_map/all_to_all | solution.py:167
  210.6 11.1 %convolution_convert_fusion.2 = bf16[512,512]{1,0:T(8,128)(2,1)} fusion(bf16[512,8192]{1,0:T(8,128)(2,1)} %get-tuple-element.47, bf16[8192,512]{1,0:T(8,128)(2,1)} %param.18), kind=kOutput, calls=%fused_computation.24 | convolution fusion | flops 4295229440 | bytes 17301504 | tf_op jit(solution)/shard_map/dot_general | solution.py:143
  221.7 5.2 %all-to-all-done.4 = bf16[16,32,512]{2,1,0:T(8,128)(2,1)S(1)} async-done(((bf16[16,32,512]{2,1,0:T(8,128)(2,1)}), bf16[16,32,512]{2,1,0:T(8,128)(2,1)S(1)}, u32[]{:S(2)}, u32[]{:S(2)}) %all-to-all-start.4) | async-done | bytes 524320 | tf_op jit(solution)/shard_map/all_to_all | solution.py:167
  226.9 4.2 %all-to-all-start.2 = ((bf16[16,32,512]{2,1,0:T(8,128)(2,1)}), bf16[16,32,512]{2,1,0:T(8,128)(2,1)}, u32[]{:S(2)}, u32[]{:S(2)}) async-start(bf16[16,32,512]{2,1,0:T(8,128)(2,1)} %bitcast.124), calls=%async_computation.2 | async-start | bytes 1048576 | tf_op jit(solution)/shard_map/all_to_all | solution.py:147
  232.5 3.4 all-reduce
  236.5 1.4 reshape.260
  237.8 1.4 gather_fusion.4
  239.3 7.4 %all-to-all-done.2 = bf16[16,32,512]{2,1,0:T(8,128)(2,1)} async-done(((bf16[16,32,512]{2,1,0:T(8,128)(2,1)}), bf16[16,32,512]{2,1,0:T(8,128)(2,1)}, u32[]{:S(2)}, u32[]{:S(2)}) %all-to-all-start.2) | async-done | bytes 524320 | tf_op jit(solution)/shard_map/all_to_all | solution.py:147
  246.7 1.4 reshape.252
  248.0 1.4 gather_fusion.2
  249.5 2.1 fusion.14
  251.6 1.2 reshape.266
  252.8 2.0 reshape.268
  254.8 1.0 fusion.10
  255.9 2.6 fusion.11
  258.5 6.6 %convert_element_type.122 = f32[256,8192]{1,0:T(8,128)} convert(bf16[256,8192]{1,0:T(8,128)(2,1)} %reduce-scatter.6.cloned.1.call-done) | non-fusion elementwise | flops 2097152 | bytes 12582912 | tf_op jit(solution)/shard_map/convert_element_type | solution.py:189
  265.1 6.2 %convert_element_type.124 = f32[8192,256]{1,0:T(8,128)} convert(bf16[8192,256]{1,0:T(8,128)(2,1)} %reduce-scatter.8.cloned.1.call-done) | non-fusion elementwise | flops 2097152 | bytes 12582912 | tf_op jit(solution)/shard_map/convert_element_type | solution.py:192
  271.3 65.5 %reduce-scatter.10.cloned.1.call-done = f32[16,2048]{1,0:T(8,128)} async-done(((f32[512,2048]{1,0:T(8,128)}), f32[16,2048]{1,0:T(8,128)}) %reduce-scatter.10.cloned.1.call-update) | async-done | bytes 131088
  (82 shorter events, 7.9 us)
Async XLA Ops:
  8.0 17.6 %copy-start = (bf16[512,1536]{1,0:T(8,128)(2,1)S(1)}, bf16[512,1536]{1,0:T(8,128)(2,1)}, u32[]{:S(2)}) copy-start(bf16[512,1536]{1,0:T(8,128)(2,1)} %param.14) | copy-start | bytes 4718596
  8.0 17.6 %copy-start.1 = (bf16[256,512]{1,0:T(8,128)(2,1)S(1)}, bf16[256,512]{1,0:T(8,128)(2,1)}, u32[]{:S(2)}) copy-start(bf16[256,512]{1,0:T(8,128)(2,1)} %param.12) | copy-start | bytes 786436
  11.5 23.8 %all-to-all-start = ((s32[16,8,1]{1,2,0:T(1,128)}), s32[16,8,1]{1,2,0:T(1,128)S(1)}, u32[]{:S(2)}, u32[]{:S(2)}) async-start(s32[16,8,1]{1,2,0:T(1,128)} %bitcast.9), calls=%async_computation | async-start | bytes 16384 | tf_op jit(solution)/shard_map/all_to_all | solution.py:137
  22.1 7.8 %copy-start.4 = (bf16[256,512]{1,0:T(8,128)(2,1)S(1)}, bf16[256,512]{1,0:T(8,128)(2,1)}, u32[]{:S(2)}) copy-start(bf16[256,512]{1,0:T(8,128)(2,1)} %param.19) | copy-start | bytes 786436
  35.3 21.6 %all-to-all-start.1 = ((bf16[16,32,512]{2,1,0:T(8,128)(2,1)}), bf16[16,32,512]{2,1,0:T(8,128)(2,1)}, u32[]{:S(2)}, u32[]{:S(2)}) async-start(bf16[16,32,512]{2,1,0:T(8,128)(2,1)} %all_to_all.36), calls=%async_computation.1 | async-start | bytes 1048576 | tf_op jit(solution)/shard_map/all_to_all | solution.py:136
  42.3 139.8 %all-reduce.4.cloned.1.call-start = ((), (), s32[]{:S(2)}) async-start(), calls=%async_computation.11 | async-start | bytes 1048576 | tf_op jit(solution)/shard_map/psum | solution.py:66
  56.9 20.6 %all-to-all-start.3 = ((bf16[16,32,512]{2,1,0:T(8,128)(2,1)}), bf16[16,32,512]{2,1,0:T(8,128)(2,1)}, u32[]{:S(2)}, u32[]{:S(2)}) async-start(bf16[16,32,512]{2,1,0:T(8,128)(2,1)} %all_to_all.41), calls=%async_computation.3 | async-start | bytes 1048576 | tf_op jit(solution)/shard_map/all_to_all | solution.py:148
  61.2 197.3 %reduce-scatter.6.cloned.1.call-start = ((), (), s32[]{:S(2)}) async-start(), calls=%async_computation.8 | async-start | bytes 12582912 | tf_op jit(solution)/shard_map/reduce_scatter | solution.py:187
  112.2 152.9 %reduce-scatter.8.cloned.1.call-start = ((), (), s32[]{:S(2)}) async-start(), calls=%async_computation.9 | async-start | bytes 12582912 | tf_op jit(solution)/shard_map/reduce_scatter | solution.py:190
  125.0 211.9 %reduce-scatter.10.cloned.1.call-start = ((), (), s32[]{:S(2)}) async-start(), calls=%async_computation.10 | async-start | bytes 4325376
  182.1 2.6 copy-start.9
  182.1 3.4 copy-start.5
  184.9 0.9 copy-start.2
  185.2 4.0 %copy-start.10 = (bf16[8,64,256]{2,1,0:T(8,128)(2,1)}, bf16[8,64,256]{2,1,0:T(8,128)(2,1)S(1)}, u32[]{:S(2)}) copy-start(bf16[8,64,256]{2,1,0:T(8,128)(2,1)S(1)} %convolution_convert_fusion.3) | copy-start | bytes 786436
  185.3 0.7 copy-start.11
  185.5 0.7 copy-start.12
  206.1 20.9 %all-to-all-start.4 = ((bf16[16,32,512]{2,1,0:T(8,128)(2,1)}), bf16[16,32,512]{2,1,0:T(8,128)(2,1)S(1)}, u32[]{:S(2)}, u32[]{:S(2)}) async-start(bf16[16,32,512]{2,1,0:T(8,128)(2,1)} %bitcast.23), calls=%async_computation.4 | async-start | bytes 1048576 | tf_op jit(solution)/shard_map/all_to_all | solution.py:167
  210.6 20.6 %copy-start.13 = (u32[32]{0:T(128)S(1)}, u32[32]{0:T(128)}, u32[]{:S(2)}) copy-start(u32[32]{0:T(128)} %constant.131) | copy-start | bytes 388
  221.7 33.2 %copy-start.3 = (bf16[8,64,256]{2,1,0:T(8,128)(2,1)S(1)}, bf16[8,64,256]{2,1,0:T(8,128)(2,1)}, u32[]{:S(2)}) copy-start(bf16[8,64,256]{2,1,0:T(8,128)(2,1)} %copy-done.2) | copy-start | bytes 786436
  221.7 33.2 %copy-start.7 = (bf16[512,512]{1,0:T(8,128)(2,1)S(1)}, bf16[512,512]{1,0:T(8,128)(2,1)}, u32[]{:S(2)}) copy-start(bf16[512,512]{1,0:T(8,128)(2,1)} %param.15) | copy-start | bytes 1572868
  221.7 34.2 %copy-start.6 = (bf16[256,512]{1,0:T(8,128)(2,1)S(1)}, bf16[256,512]{1,0:T(8,128)(2,1)}, u32[]{:S(2)}) copy-start(bf16[256,512]{1,0:T(8,128)(2,1)} %param.19) | copy-start | bytes 786436
  226.9 8.9 %copy-start.8 = (bf16[16,32,512]{2,1,0:T(8,128)(2,1)}, bf16[16,32,512]{2,1,0:T(8,128)(2,1)S(1)}, u32[]{:S(2)}) copy-start(bf16[16,32,512]{2,1,0:T(8,128)(2,1)S(1)} %all-to-all-done.4) | copy-start | bytes 1572868
  226.9 19.8 %all-to-all-start.2 = ((bf16[16,32,512]{2,1,0:T(8,128)(2,1)}), bf16[16,32,512]{2,1,0:T(8,128)(2,1)}, u32[]{:S(2)}, u32[]{:S(2)}) async-start(bf16[16,32,512]{2,1,0:T(8,128)(2,1)} %bitcast.124), calls=%async_computation.2 | async-start | bytes 1048576 | tf_op jit(solution)/shard_map/all_to_all | solution.py:147
Sparse Core Ops, SparseCore 0:
  49.2 132.8 all-reduce.3
Sparse Core Ops, SparseCore 1:
  112.3 17.9 reduce-scatter.5
  132.4 18.0 reduce-scatter.7
  194.9 141.8 reduce-scatter.9
where the time goes:
time: 351 us; the launch traced here: 345 us
  waiting for transfers between devices  142 us (40%)
  matrix products  97.8 us (28%)
  local copies, waits for them, and re-layouts  32.1 us (9%)
  starting transfers between devices  28.6 us (8%)
  other arithmetic  23.9 us (7%)
  between operations  17.2 us (5%)
    unnamed x5, waiting for transfers between devices  65.6 us
    psum x1, waiting for transfers between devices, on_device(): lax.psum((local_summary, local_grad), ('wide', 'narrow'))  57.1 us
    dot_general x1, matrix products, on_device(): jnp.einsum('rd,sd->rs', recv_cots, w_expert_out, preferred_element_type=j...  23.2 us
    dot_general x1, matrix products, on_device(): jnp.dot(recv_feats, w_expert_in, preferred_element_type=jnp.float32)  16.2 us
    convert_element_type x3, other arithmetic, on_device(): grad_in, grad_out_w, grad_bias_out = (lax.psum_scatter(grad_first.astype(...  13.5 us
    dot_general x1, matrix products, on_device(): jnp.einsum('rs,rd->sd', hidden, recv_cots, preferred_element_type=jnp.flo...  12.7 us
    dot_general x1, matrix products, on_device(): jnp.einsum('rd,rs->ds', recv_feats, grad_pre, preferred_element_type=jnp....  11.4 us
    dot_general x1, matrix products, on_device(): jnp.einsum('rs,ds->rd', grad_pre, w_expert_in, preferred_element_type=jnp...  11.2 us
  transfers between devices with their start and end apart: 9, of which 5 were waited for; matrix products, arithmetic and copies ran while one was open for 42% of the time, Pallas kernels for 0%

commit v1 on v0

v1 whole, which is shorter than its diff:
```python
import functools

import jax
import jax.numpy as jnp
from jax import lax
from jax.experimental import pallas as pl
from jax.experimental.pallas import tpu as pltpu
from jax.sharding import PartitionSpec as P

HEADS = 8
HID = 2048
DOMAIN_SPECIALS = 64
DOMAIN_REPEAT_CAP = 2

gelu_scale = 0.7978845608
gelu_cubic = 0.044715

F32 = jnp.float32
BF16 = jnp.bfloat16
VMEM_SPEC = pl.BlockSpec(memory_space=pltpu.VMEM)


def dot(a, b, ca=1, cb=0):
    return lax.dot_general(a, b, (((ca,), (cb,)), ((), ())), preferred_element_type=F32)


def dot_split(a, b):
    high = a.astype(BF16)
    low = (a - high.astype(F32)).astype(BF16)
    return dot(high, b) + dot(low, b)


def head_mask(width, head_dim):
    rows = lax.broadcasted_iota(jnp.int32, (width, width), 0) // head_dim
    cols = lax.broadcasted_iota(jnp.int32, (width, width), 1) // head_dim
    return rows == cols


def params(flops, size, vmem=48):
    return dict(
        cost_estimate=pl.CostEstimate(flops=flops, bytes_accessed=size, transcendentals=0),
        compiler_params=pltpu.CompilerParams(vmem_limit_bytes=vmem * 2**20),
    )


def pack_kernel(block_len, owner_count, experts_here, col_ref, row_ref, x_ref, cot_ref, pick_ref, out_ref):
    rows, points = pick_ref.shape
    width = x_ref.shape[1]
    slot_rows = experts_here * DOMAIN_REPEAT_CAP * block_len
    col, row = col_ref[...], row_ref[...]
    first = lax.broadcasted_iota(jnp.int32, (points, points), 0)
    second = lax.broadcasted_iota(jnp.int32, (points, points), 1)
    earlier = (col == row) & (first // block_len < second // block_len) & (first % block_len == 0)
    rank = jnp.sum(earlier.astype(jnp.int32), axis=0, keepdims=True)
    slot = lax.broadcasted_iota(jnp.int32, (rows, 1), 0)
    dest = slot // slot_rows
    inner = slot % slot_rows
    expert = inner // (DOMAIN_REPEAT_CAP * block_len)
    region = (dest // owner_count) * experts_here + expert
    place = (inner // block_len) % DOMAIN_REPEAT_CAP
    lane = lax.broadcasted_iota(jnp.int32, (1, points), 1) % block_len
    want = (region * DOMAIN_REPEAT_CAP + place) * block_len + slot % block_len
    have = (row * DOMAIN_REPEAT_CAP + rank) * block_len + lane
    pick = jnp.where(want == have, 1.0, 0.0).astype(BF16)
    pick_ref[...] = pick
    out_ref[:, :width] = dot(pick, x_ref[...]).astype(BF16)
    out_ref[:, width:] = dot(pick, cot_ref[...]).astype(BF16)


def first_kernel(
    total, x_ref, wqkv_ref, wout_ref, cot_ref,
    q_ref, kn_ref, vn_ref, ku_ref, vu_ref, ks_ref, vs_ref, gm_ref, sums_ref,
):
    width = x_ref.shape[1]
    head_dim = width // HEADS
    mask = head_mask(width, head_dim)
    mean_mat = jnp.where(mask, 1.0 / head_dim, 0.0).astype(BF16)

    def normalize(raw):
        centred = raw.astype(F32) - dot(raw, mean_mat)
        scale = jnp.sqrt(dot_split(centred * centred, mean_mat) + 1e-05)
        return centred / scale, scale

    def fold(full):
        kept = jnp.where(mask, full, 0.0) * (1.0 / total)
        return jnp.sum(kept.reshape(HEADS, head_dim, width), axis=0)

    x = x_ref[...]
    q = dot(x, wqkv_ref[:, :width]).astype(BF16)
    k_unit, k_scale = normalize(dot(x, wqkv_ref[:, width : 2 * width]).astype(BF16))
    v_unit, v_scale = normalize(dot(x, wqkv_ref[:, 2 * width :]).astype(BF16))
    grad_mixed = dot(cot_ref[...], wout_ref[...], 1, 1).astype(BF16)
    k_norm, v_norm = k_unit.astype(BF16), v_unit.astype(BF16)
    both = jnp.concatenate([fold(dot(k_norm, v_norm, 0, 0)), fold(dot(q, grad_mixed, 0, 0))], axis=0)
    tall = both.shape[0]
    for piece in range(width // 128):
        sums_ref[piece * tall : (piece + 1) * tall, :] = both[:, piece * 128 : (piece + 1) * 128]
    q_ref[...] = q
    kn_ref[...] = k_norm
    vn_ref[...] = v_norm
    ku_ref[...] = k_unit
    vu_ref[...] = v_unit
    ks_ref[...] = k_scale
    vs_ref[...] = v_scale
    gm_ref[...] = grad_mixed


def second_kernel(
    total, sums_ref, x_ref, wqkv_ref, wout_ref, cot_ref,
    q_ref, kn_ref, vn_ref, ku_ref, vu_ref, ks_ref, vs_ref, gm_ref,
    att_ref, out_ref, back_ref,
):
    width = x_ref.shape[1]
    head_dim = width // HEADS
    mask = head_mask(width, head_dim)
    mean_mat = jnp.where(mask, 1.0 / head_dim, 0.0).astype(BF16)
    tall = sums_ref.shape[0] // (width // 128)
    both = jnp.concatenate([sums_ref[p * tall : (p + 1) * tall, :] for p in range(width // 128)], axis=1)

    def spread(folded):
        whole = jnp.concatenate([folded] * HEADS, axis=0)
        return jnp.where(mask, whole, 0.0).astype(BF16)

    summary = spread(both[:head_dim])
    grad_summary = spread(both[head_dim:])

    def back(grad, unit, scale):
        mean_grad = dot_split(grad, mean_mat)
        mean_cross = dot_split(grad * unit, mean_mat)
        return ((grad - mean_grad - unit * mean_cross) / scale).astype(BF16)

    x, cot = x_ref[...], cot_ref[...]
    mixed = dot(q_ref[...], summary).astype(BF16)
    grad_query = dot(gm_ref[...], summary, 1, 1).astype(BF16)
    grad_key = back(dot(vn_ref[...], grad_summary, 1, 1), ku_ref[...], ks_ref[...])
    grad_value = back(dot(kn_ref[...], grad_summary), vu_ref[...], vs_ref[...])
    scale = 1.0 / total
    x_turned = x.T
    att_ref[:, :width] = (dot(x_turned, grad_query) * scale).astype(BF16)
    att_ref[:, width : 2 * width] = (dot(x_turned, grad_key) * scale).astype(BF16)
    att_ref[:, 2 * width : 3 * width] = (dot(x_turned, grad_value) * scale).astype(BF16)
    att_ref[:, 3 * width :] = (dot(mixed, cot, 0, 0) * scale).astype(BF16)
    out_ref[...] = x.astype(F32) + dot(mixed, wout_ref[...])
    back_ref[...] = (
        cot.astype(F32)
        + dot(grad_query, wqkv_ref[:, :width], 1, 1)
        + dot(grad_key, wqkv_ref[:, width : 2 * width], 1, 1)
        + dot(grad_value, wqkv_ref[:, 2 * width :], 1, 1)
    )


def expert_kernel(
    share, half_ref, feat_ref, cot_ref, feat_half_ref, cot_half_ref, win_ref, bias_ref, wout_ref,
    ret_ref, gin_ref, gout_ref, gbias_ref, out_acc, back_acc,
):
    step = pl.program_id(1)
    own, width = out_acc.shape
    w_in, w_out = win_ref[...], wout_ref[...]
    pre = dot(feat_ref[0], w_in) + bias_ref[...]
    grad_hidden = dot(cot_ref[0], w_out, 1, 1)
    square = pre * pre
    tangent = jnp.tanh(gelu_scale * (pre + gelu_cubic * square * pre))
    half_sum = 0.5 * (1.0 + tangent)
    hidden = (pre * half_sum).astype(BF16)
    slope = half_sum + 0.5 * pre * (1.0 - tangent * tangent) * gelu_scale * (1.0 + 3.0 * gelu_cubic * square)
    grad_pre = (grad_hidden * slope).astype(BF16)
    out_part = dot(hidden[:own], w_out)
    back_part = dot(grad_pre[:own], w_in, 1, 1)

    @pl.when(step == 0)
    def _():
        out_acc[...] = out_part
        back_acc[...] = back_part

    @pl.when(step > 0)
    def _():
        out_acc[...] += out_part
        back_acc[...] += back_part

    gin_ref[...] = dot(feat_half_ref[0], grad_pre, 0, 0) * share
    gout_ref[...] = dot(hidden, cot_half_ref[0], 0, 0) * share
    gbias_ref[...] = jnp.sum(grad_pre.astype(F32), axis=0, keepdims=True) * share

    @pl.when(step == pl.num_programs(1) - 1)
    def _():
        ret_ref[0, :, :width] = out_acc[...].astype(BF16)
        ret_ref[0, :, width:] = back_acc[...].astype(BF16)


def final_kernel(pick_ref, ret_ref, out_base_ref, back_base_ref, out_ref, back_ref):
    width = out_ref.shape[1]
    picked = dot(pick_ref[...], ret_ref[...], 0, 0)
    out_ref[...] = (out_base_ref[...] + picked[:, :width]).astype(BF16)
    back_ref[...] = (back_base_ref[...] + picked[:, width:]).astype(BF16)


def on_device(
    point_feats, region_ids, w_qkv, w_out, w_expert_in, b_expert_in, w_expert_out, out_cotangent
):
    wide_count = lax.axis_size("wide")
    narrow_count = lax.axis_size("narrow")
    device_count = wide_count * narrow_count
    narrow_index = lax.axis_index("narrow")
    swap = [(i, (i + 1) % narrow_count) for i in range(narrow_count)]
    points, width = point_feats.shape
    total = points * device_count
    blocks = region_ids.shape[0]
    block_len = points // blocks
    slab = w_expert_in.shape[1]
    owner_count = max(1, wide_count // DOMAIN_SPECIALS)
    experts_here = max(1, DOMAIN_SPECIALS // wide_count)
    hid_here = slab // experts_here
    slot_rows = DOMAIN_REPEAT_CAP * block_len
    rows = wide_count * experts_here * slot_rows
    own = rows // experts_here

    labels = jnp.repeat(region_ids, block_len)
    pick, packed = pl.pallas_call(
        functools.partial(pack_kernel, block_len, owner_count, experts_here),
        out_shape=(
            jax.ShapeDtypeStruct((rows, points), BF16),
            jax.ShapeDtypeStruct((rows, 2 * width), BF16),
        ),
        in_specs=[VMEM_SPEC] * 4,
        out_specs=[VMEM_SPEC] * 2,
        name="pack",
        **params(4 * rows * points * width, 4 * rows * width),
    )(labels[:, None], labels[None, :], point_feats, out_cotangent)
    received = lax.all_to_all(packed, "wide", split_axis=0, concat_axis=0, tiled=True)

    wide_bf = jax.ShapeDtypeStruct((points, width), BF16)
    wide_f = jax.ShapeDtypeStruct((points, width), F32)
    fold_rows = 2 * (width // HEADS) * (width // 128)
    *kept, sums = pl.pallas_call(
        functools.partial(first_kernel, total),
        out_shape=(
            wide_bf, wide_bf, wide_bf, wide_f, wide_f, wide_f, wide_f, wide_bf,
            jax.ShapeDtypeStruct((fold_rows, 128), F32),
        ),
        in_specs=[VMEM_SPEC] * 4,
        out_specs=[VMEM_SPEC] * 9,
        name="first",
        **params(20 * points * width * width, 8 * points * width),
    )(point_feats, w_qkv, w_out, out_cotangent)
    axes = ("wide", "narrow")
    pieces = lax.all_to_all(sums, axes, split_axis=0, concat_axis=0, tiled=True)
    piece = jnp.sum(pieces.reshape(device_count, fold_rows // device_count, 128), axis=0)
    copies = jnp.broadcast_to(piece[None], (device_count,) + piece.shape).reshape(fold_rows, 128)
    sums = lax.all_to_all(copies, axes, split_axis=0, concat_axis=0, tiled=True)
    att, out_base, back_base = pl.pallas_call(
        functools.partial(second_kernel, total),
        out_shape=(jax.ShapeDtypeStruct((width, 4 * width), BF16), wide_f, wide_f),
        in_specs=[VMEM_SPEC] * 13,
        out_specs=[VMEM_SPEC] * 3,
        name="second",
        **params(30 * points * width * width, 8 * points * width),
    )(sums, point_feats, w_qkv, w_out, out_cotangent, *kept)
    att = att.reshape(wide_count, narrow_count, width // device_count, 4 * width)
    mine = lax.dynamic_index_in_dim(att, narrow_index, 1, keepdims=False)
    for shift in range(1, narrow_count):
        other = lax.rem(narrow_index + shift, narrow_count)
        theirs = lax.dynamic_index_in_dim(att, other, 1, keepdims=False)
        perm = [(i, (i + shift) % narrow_count) for i in range(narrow_count)]
        mine = mine.astype(F32) + lax.ppermute(theirs, "narrow", perm).astype(F32)
    mine = mine.astype(BF16).reshape(wide_count * (width // device_count), 4 * width)
    att_parts = lax.all_to_all(mine, "wide", split_axis=0, concat_axis=0, tiled=True)
    grad_attention = jnp.sum(
        att_parts.reshape(wide_count, width // device_count, 4 * width).astype(F32), axis=0
    )

    parts = [received]
    for shift in range(1, narrow_count):
        perm = [(i, (i + shift) % narrow_count) for i in range(narrow_count)]
        parts.append(lax.ppermute(received, "narrow", perm))
    by_expert = [
        part.reshape(wide_count, experts_here, slot_rows, 2 * width)
        .transpose(1, 0, 2, 3)
        .reshape(experts_here, own, 2 * width)
        for part in parts
    ]
    gathered = jnp.concatenate(by_expert, axis=1)
    all_rows = own * narrow_count
    tile = min(512, hid_here)
    steps = hid_here // tile
    half = width // narrow_count
    share = DOMAIN_SPECIALS / total
    returned, grad_in, grad_out_w, grad_bias = pl.pallas_call(
        functools.partial(expert_kernel, share),
        out_shape=(
            jax.ShapeDtypeStruct((experts_here, own, 2 * width), BF16),
            jax.ShapeDtypeStruct((half, slab), F32),
            jax.ShapeDtypeStruct((slab, half), F32),
            jax.ShapeDtypeStruct((1, slab), F32),
        ),
        grid_spec=pltpu.PrefetchScalarGridSpec(
            num_scalar_prefetch=1,
            grid=(experts_here, steps),
            in_specs=[
                pl.BlockSpec((1, all_rows, width), lambda e, t, n: (e, 0, 0)),
                pl.BlockSpec((1, all_rows, width), lambda e, t, n: (e, 0, 1)),
                pl.BlockSpec((1, all_rows, half), lambda e, t, n: (e, 0, n[0])),
                pl.BlockSpec((1, all_rows, half), lambda e, t, n: (e, 0, narrow_count + n[0])),
                pl.BlockSpec((width, tile), lambda e, t, n: (0, e * steps + t)),
                pl.BlockSpec((1, tile), lambda e, t, n: (0, e * steps + t)),
                pl.BlockSpec((tile, width), lambda e, t, n: (e * steps + t, 0)),
            ],
            out_specs=[
                pl.BlockSpec((1, own, 2 * width), lambda e, t, n: (e, 0, 0)),
                pl.BlockSpec((half, tile), lambda e, t, n: (0, e * steps + t)),
                pl.BlockSpec((tile, half), lambda e, t, n: (e * steps + t, 0)),
                pl.BlockSpec((1, tile), lambda e, t, n: (0, e * steps + t)),
            ],
            scratch_shapes=[pltpu.VMEM((own, width), F32), pltpu.VMEM((own, width), F32)],
        ),
        name="experts",
        **params(8 * all_rows * width * slab, 8 * width * slab),
    )(
        narrow_index.astype(jnp.int32)[None],
        gathered, gathered, gathered, gathered,
        w_expert_in, b_expert_in[None, :], w_expert_out,
    )
    returned = (
        returned.reshape(experts_here, wide_count, slot_rows, 2 * width)
        .transpose(1, 0, 2, 3)
        .reshape(rows, 2 * width)
    )
    returned = lax.all_to_all(returned, "wide", split_axis=0, concat_axis=0, tiled=True)
    layer_out, grad_feats = pl.pallas_call(
        final_kernel,
        out_shape=(wide_bf, wide_bf),
        in_specs=[VMEM_SPEC] * 4,
        out_specs=[VMEM_SPEC] * 2,
        name="final",
        **params(4 * rows * points * width, 4 * rows * width),
    )(pick, returned, out_base, back_base)
    bias_half = slab // narrow_count
    grad_bias_out = lax.dynamic_slice_in_dim(grad_bias[0], narrow_index * bias_half, bias_half, 0)
    return (layer_out, grad_feats, grad_attention, grad_in, grad_out_w, grad_bias_out)


def solution(mesh):
    placed = (
        P(("wide", "narrow"), None),
        P(("wide", "narrow")),
        P(),
        P(),
        P(None, "wide"),
        P("wide"),
        P("wide", None),
        P(("wide", "narrow"), None),
    )
    return jax.shard_map(
        on_device,
        mesh=mesh,
        in_specs=placed,
        out_specs=(
            P(("wide", "narrow"), None),
            P(("wide", "narrow"), None),
            P(("wide", "narrow"), None),
            P("narrow", "wide"),
            P("wide", "narrow"),
            P(("wide", "narrow")),
        ),
        check_vma=False,
    )
```

time: 351 us -> 145 us (0.41); the launches traced: 345 us -> 144 us
  waiting for transfers between devices: 142 us -> 41.8 us
  matrix products: 97.8 us -> 0 us
  Pallas kernels: 0 us -> 34.9 us
  other arithmetic: 23.9 us -> 3.61 us
  between operations: 17.2 us -> 0.84 us
  blocking collectives: 3.36 us -> 17.7 us
  starting transfers between devices: 28.6 us -> 20.1 us
  local copies, waits for them, and re-layouts: 32.1 us -> 24.8 us
    dot_general x18 -> x0, matrix products: 97.8 us -> none  [the longest x1 23.2 us: on_device(): jnp.einsum('rd,sd->rs', recv_cots, w_expert_out, preferred_element_type=j...]
    unnamed x5 -> x0, waiting for transfers between devices: 65.6 us -> none
    psum x1 -> x0, waiting for transfers between devices: 57.1 us -> none  [on_device(): lax.psum((local_summary, local_grad), ('wide', 'narrow'))]
    pallas_call x0 -> x5, Pallas kernels: none -> 34.9 us  [the longest x1 24.5 us: on_device(): pl.pallas_call(functools.partial(expert_kernel, share), out_shape=(jax.Sh...]
    all_to_all x5 -> x4, waiting for transfers between devices: 19.3 us -> 41.8 us  [the longest x1 23.1 us: on_device(): lax.all_to_all(returned, 'wide', split_axis=0, concat_axis=0, tiled=True)]
    all_to_all x0 -> x1, blocking collectives: none -> 17.7 us  [on_device(): pieces = lax.all_to_all(sums, axes, split_axis=0, concat_axis=0, tiled=True)]
    convert_element_type x7 -> x1, other arithmetic: 14.9 us -> 2.6 us  [on_device(): mine.astype(BF16).reshape(wide_count * (width // device_count), 4 * width)]
    unnamed x30 -> x48, local copies, waits for them, and re-layouts: 6.63 us -> 17.1 us
  transfers between devices with their start and end apart: 9 -> 6, of which waited for: 5 -> 3; matrix products, arithmetic and copies ran while one was open for 42% -> 7% of each run, Pallas kernels for 0% -> 22%
where the time goes in v1:
time: 145 us; the launch traced here: 144 us
  waiting for transfers between devices  41.8 us (29%)
  Pallas kernels  34.9 us (24%)
  local copies, waits for them, and re-layouts  24.8 us (17%)
  starting transfers between devices  20.1 us (14%)
  blocking collectives  17.7 us (12%)
  other arithmetic  3.61 us (2%)
    pallas_call x1, Pallas kernels, on_device(): pl.pallas_call(functools.partial(expert_kernel, share), out_shape=(jax.Sh...  24.5 us
    all_to_all x1, waiting for transfers between devices, on_device(): lax.all_to_all(returned, 'wide', split_axis=0, concat_axis=0, tiled=True)  23.1 us
    all_to_all x1, blocking collectives, on_device(): pieces = lax.all_to_all(sums, axes, split_axis=0, concat_axis=0, tiled=True)  17.7 us
    unnamed x48, local copies, waits for them, and re-layouts  17.1 us
    all_to_all x1, waiting for transfers between devices, on_device(): lax.all_to_all(packed, 'wide', split_axis=0, concat_axis=0, tiled=True)  9.95 us
    all_to_all x1, waiting for transfers between devices, on_device(): sums = lax.all_to_all(copies, axes, split_axis=0, concat_axis=0, tiled=True)  8.7 us
    all_to_all x1, starting transfers between devices, on_device(): lax.all_to_all(returned, 'wide', split_axis=0, concat_axis=0, tiled=True)  6.91 us
    all_to_all x1, starting transfers between devices, on_device(): lax.all_to_all(mine, 'wide', split_axis=0, concat_axis=0, tiled=True)  6.23 us
  transfers between devices with their start and end apart: 6, of which 3 were waited for; matrix products, arithmetic and copies ran while one was open for 7% of the time, Pallas kernels for 22%

profile of v1, /device:TPU:0, one launch (start us, length us, event | category | flops | bytes accessed | tf_op | source)
XLA Modules:
  0.0 143.8 jit_solution(4751402471430360618)
XLA Ops:
  0.6 0.0 copy-start
  0.6 1.4 copy-done
  2.0 1.0 copy-done.1
  3.1 0.9 copy-done.3
  4.0 0.9 copy-done.5
  5.0 2.5 %first.1 = (bf16[256,512]{1,0:T(8,128)(2,1)S(1)}, bf16[256,512]{1,0:T(8,128)(2,1)S(1)}, bf16[256,512]{1,0:T(8,128)(2,1)S(1)}, f32[256,512]{1,0:T(8,128)S(1)}, f3...) custom-call(bf16[256,512]{1,0:T(8,128)(2,1)S(1)} %copy-done.3, ...), custom_call_target="tpu_custom_call" | custom-call | flops 1342177280 | bytes 1048576 | tf_op jit(solution)/shard_map/first/pallas_call | solution.py:234
  7.5 0.0 copy-start.8
  7.5 0.8 copy-done.8
  8.3 0.8 copy-done.10
  9.1 0.8 copy-done.12
  9.9 0.7 copy-done.14
  10.6 0.7 copy-done.16
  11.3 0.7 copy-done.18
  12.0 0.7 copy-done.20
  12.7 17.7 %all_to_all.46 = f32[32,16,128]{2,1,0:T(8,128)S(1)} all-to-all(f32[32,16,128]{2,1,0:T(8,128)S(1)} %bitcast.36), channel_id=1, replica_groups=mesh['wide'=16,'narrow'=2] {'wide','narrow'}, dimensions={0} | all-to-all | bytes 524288 | tf_op jit(solution)/shard_map/all_to_all | solution.py:246
  30.4 0.0 copy-start.2
  30.5 0.7 broadcast_in_dim.18
  31.2 2.6 %all-to-all-start.3 = ((f32[32,16,128]{2,1,0:T(8,128)}), f32[32,16,128]{2,1,0:T(8,128)S(1)}, u32[]{:S(2)}, u32[]{:S(2)}) async-start(f32[32,16,128]{2,1,0:T(8,128)} %broadcast_in_dim.18), calls=%async_computation.3 | async-start | bytes 524288 | tf_op jit(solution)/shard_map/all_to_all | solution.py:249
  33.8 0.1 broadcast_in_dim.15
  33.9 0.1 broadcast_in_dim_reshape.8.col_ref
  34.0 0.1 broadcast_in_dim_reshape.7.row_ref
  34.1 1.6 %pack.1 = (bf16[512,256]{1,0:T(8,128)(2,1)S(1)}, bf16[512,1024]{1,0:T(8,128)(2,1)}) custom-call(s32[256,1]{1,0:T(8,128)S(1)} %broadcast_in_dim_reshape.8.col_ref, s32[1,256]{1,0:T(1,128)S(1)} %broadcast_in_dim_reshape.7.row_ref, bf16[256,512]{1,0:T(8,128)(2,1)S(1)} %copy-done.4, bf16[256,512]{1,0:T(8,128)(2,1)S(1)} %copy-done.6), custom_call_target="tpu_custom_call" | custom-call | flops 268435456 | bytes 1048576 | tf_op jit(solution)/shard_map/pack/pallas_call | solution.py:218
  35.7 8.7 %all-to-all-done.3 = f32[32,16,128]{2,1,0:T(8,128)S(1)} async-done(((f32[32,16,128]{2,1,0:T(8,128)}), f32[32,16,128]{2,1,0:T(8,128)S(1)}, u32[]{:S(2)}, u32[]{:S(2)}) %all-to-all-start.3) | async-done | bytes 262176 | tf_op jit(solution)/shard_map/all_to_all | solution.py:249
  44.4 4.3 %all-to-all-start = ((bf16[16,32,1024]{2,1,0:T(8,128)(2,1)}), bf16[16,32,1024]{2,1,0:T(8,128)(2,1)}, u32[]{:S(2)}, u32[]{:S(2)}) async-start(bf16[16,32,1024]{2,1,0:T(8,128)(2,1)} %bitcast.1), calls=%async_computation | async-start | bytes 2097152 | tf_op jit(solution)/shard_map/all_to_all | solution.py:229
  48.7 0.0 copy-start.9
  48.8 1.0 copy-done.9
  49.8 1.0 copy-done.11
  50.8 1.0 copy-done.13
  51.9 0.9 copy-done.15
  52.8 0.9 copy-done.17
  53.8 0.9 copy-done.19
  54.7 0.9 copy-done.21
  55.7 5.2 %second.1 = (bf16[512,2048]{1,0:T(8,128)(2,1)}, f32[256,512]{1,0:T(8,128)S(1)}, f32[256,512]{1,0:T(8,128)S(1)}) custom-call(f32[512,128]{1,0:T(8,128)S(1)} %bitcast.35, bf16[256,512]{1,0:T(8,128)(2,1)S(1)} %copy-done.4, bf16[512,1536]{1,0:T(8,128)(2,1)} %wqkv_ref.3, bf16[512,512]{1,0:T(8,128)(2,1)S(1)} %copy-done.2, bf16[256,512]{1,0:T(8,128)(2,1)S(1)} %copy-done.6, ...), custom_call_target="tpu_custom_call" | custom-call | flops 2013265920 | bytes 1048576 | tf_op jit(solution)/shard_map/second/pallas_call | solution.py:250
  60.9 2.5 %dynamic-slice_bitcast_fusion = bf16[16,16,2048]{2,1,0:T(8,128)(2,1)} fusion(bf16[16,2,16,2048]{3,2,1,0:T(8,128)(2,1)} %bitcast.39, s32[]{:T(128)S(6)} %select_n.11), kind=kLoop, calls=%fused_computation.7 | loop fusion | bytes 2097156 | tf_op jit(solution)/shard_map/jit(dynamic_index_in_dim)/squeeze | solution.py:262
  63.4 9.9 %all-to-all-done = bf16[16,32,1024]{2,1,0:T(8,128)(2,1)} async-done(((bf16[16,32,1024]{2,1,0:T(8,128)(2,1)}), bf16[16,32,1024]{2,1,0:T(8,128)(2,1)}, u32[]{:S(2)}, u32[]{:S(2)}) %all-to-all-start) | async-done | bytes 1048608 | tf_op jit(solution)/shard_map/all_to_all | solution.py:229
  73.3 2.6 %fusion = bf16[16,16,2048]{2,1,0:T(8,128)(2,1)} fusion(bf16[16,16,2048]{2,1,0:T(8,128)(2,1)} %collective-permute-done.1, bf16[16,2,16,2048]{3,2,1,0:T(8,128)(2,1)S(1)} %bitcast.40, s32[]{:T(128)S(6)} %select_n.10), kind=kLoop, calls=%fused_computation.2 | loop fusion | flops 2097152 | bytes 3145732 | tf_op jit(solution)/shard_map/convert_element_type | solution.py:265
  75.9 6.2 %all-to-all-start.4 = ((bf16[16,16,2048]{2,1,0:T(8,128)(2,1)}), bf16[16,16,2048]{2,1,0:T(8,128)(2,1)S(1)}, u32[]{:S(2)}, u32[]{:S(2)}) async-start(bf16[16,16,2048]{2,1,0:T(8,128)(2,1)} %fusion), calls=%async_computation.4 | async-start | bytes 2097152 | tf_op jit(solution)/shard_map/all_to_all | solution.py:266
  82.2 1.3 copy_bitcast_fusion.2
  83.5 1.3 copy.22
  84.8 0.2 pad_maximum_fusion.feat_ref.cot_ref.feat_half_ref.cot_half_ref
  85.0 0.6 copy-done.7
  85.6 24.5 %experts.1 = (bf16[4,128,1024]{2,1,0:T(8,128)(2,1)S(1)}, f32[256,8192]{1,0:T(8,128)}, f32[8192,256]{1,0:T(8,128)}, f32[1,8192]{1,0:T(1,128)S(1)}) custom-call(s32[1]{0:T(128)} %bitcast.half_ref, bf16[4,256,1024]{2,1,0:T(8,128)(2,1)S(1)} %pad_maximum_fusion.feat_ref.cot_ref.feat_half_ref.cot_half_ref, ...), custom_call_target="tpu_custom_call" | custom-call | flops 8589934592 | bytes 33554432 | tf_op jit(solution)/shard_map/experts/pallas_call | solution.py:287
  110.1 1.1 copy_bitcast_fusion
  111.1 6.9 %all-to-all-start.1 = ((bf16[16,32,1024]{2,1,0:T(8,128)(2,1)}), bf16[16,32,1024]{2,1,0:T(8,128)(2,1)S(1)}, u32[]{:S(2)}, u32[]{:S(2)}) async-start(bf16[16,32,1024]{2,1,0:T(8,128)(2,1)} %copy_bitcast_fusion), calls=%async_computation.1 | async-start | bytes 2097152 | tf_op jit(solution)/shard_map/all_to_all | solution.py:327
  118.0 0.6 constant_dynamic-slice_fusion
  118.7 0.8 convert_reduce_fusion
  119.5 23.1 %all-to-all-done.1 = bf16[16,32,1024]{2,1,0:T(8,128)(2,1)S(1)} async-done(((bf16[16,32,1024]{2,1,0:T(8,128)(2,1)}), bf16[16,32,1024]{2,1,0:T(8,128)(2,1)S(1)}, u32[]{:S(2)}, u32[]{:S(2)}) %all-to-all-start.1) | async-done | bytes 1048608 | tf_op jit(solution)/shard_map/all_to_all | solution.py:327
  142.6 1.2 final.1
  (31 shorter events, 0.1 us)
Async XLA Ops:
  0.6 1.4 copy-start
  2.0 1.0 copy-start.1
  3.1 0.9 copy-start.3
  4.0 0.9 copy-start.5
  5.0 28.8 %copy-start.23 = (s32[64]{0:T(128)S(1)}, s32[64]{0:T(128)}, u32[]{:S(2)}) copy-start(s32[64]{0:T(128)} %param.9) | copy-start | bytes 772
  5.0 29.1 %copy-start.4 = (bf16[256,512]{1,0:T(8,128)(2,1)S(1)}, bf16[256,512]{1,0:T(8,128)(2,1)}, u32[]{:S(2)}) copy-start(bf16[256,512]{1,0:T(8,128)(2,1)} %x_ref.5) | copy-start | bytes 786436
  5.0 29.1 %copy-start.6 = (bf16[256,512]{1,0:T(8,128)(2,1)S(1)}, bf16[256,512]{1,0:T(8,128)(2,1)}, u32[]{:S(2)}) copy-start(bf16[256,512]{1,0:T(8,128)(2,1)} %cot_ref.5) | copy-start | bytes 786436
  7.5 0.8 copy-start.8
  8.3 0.8 copy-start.10
  9.1 0.8 copy-start.12
  9.9 0.7 copy-start.14
  10.6 0.7 copy-start.16
  11.3 0.7 copy-start.18
  12.0 0.7 copy-start.20
  30.4 18.3 %copy-start.2 = (bf16[512,512]{1,0:T(8,128)(2,1)S(1)}, bf16[512,512]{1,0:T(8,128)(2,1)}, u32[]{:S(2)}) copy-start(bf16[512,512]{1,0:T(8,128)(2,1)} %wout_ref.5) | copy-start | bytes 1572868
  31.2 13.2 %all-to-all-start.3 = ((f32[32,16,128]{2,1,0:T(8,128)}), f32[32,16,128]{2,1,0:T(8,128)S(1)}, u32[]{:S(2)}, u32[]{:S(2)}) async-start(f32[32,16,128]{2,1,0:T(8,128)} %broadcast_in_dim.18), calls=%async_computation.3 | async-start | bytes 524288 | tf_op jit(solution)/shard_map/all_to_all | solution.py:249
  44.4 29.0 %all-to-all-start = ((bf16[16,32,1024]{2,1,0:T(8,128)(2,1)}), bf16[16,32,1024]{2,1,0:T(8,128)(2,1)}, u32[]{:S(2)}, u32[]{:S(2)}) async-start(bf16[16,32,1024]{2,1,0:T(8,128)(2,1)} %bitcast.1), calls=%async_computation | async-start | bytes 2097152 | tf_op jit(solution)/shard_map/all_to_all | solution.py:229
  48.7 1.0 copy-start.9
  49.8 1.0 copy-start.11
  50.8 1.0 copy-start.13
  51.9 0.9 copy-start.15
  52.8 0.9 copy-start.17
  53.8 0.9 copy-start.19
  54.7 0.9 copy-start.21
  60.9 12.4 %copy-start.22 = (bf16[512,2048]{1,0:T(8,128)(2,1)S(1)}, bf16[512,2048]{1,0:T(8,128)(2,1)}, u32[]{:S(2)}) copy-start(bf16[512,2048]{1,0:T(8,128)(2,1)} %get-tuple-element.42) | copy-start | bytes 6291460
  63.4 10.0 %collective-permute-start.1 = (bf16[16,16,2048]{2,1,0:T(8,128)(2,1)}, bf16[16,16,2048]{2,1,0:T(8,128)(2,1)}, u32[]{:S(2)}, u32[]{:S(2)}) collective-permute-start(bf16[16,16,2048]{2,1,0:T(8,128)(2,1)} %dynamic-slice_bitcast_fusion), channel_id=1, source_target_pairs={{0,1},{1,0},{2,3},{3,2},{4,5},{5,4},{6,7},{7,6},{8,9},{9,8},{10,11... | collective-permute-start | bytes 3145736 | tf_op jit(solution)/shard_map/ppermute | solution.py:264
  73.3 10.2 %collective-permute-start = (bf16[512,1024]{1,0:T(8,128)(2,1)}, bf16[512,1024]{1,0:T(8,128)(2,1)}, u32[]{:S(2)}, u32[]{:S(2)}) collective-permute-start(bf16[512,1024]{1,0:T(8,128)(2,1)} %bitcast.5), channel_id=1, source_target_pairs={{0,1},{1,0},{2,3},{3,2},{4,5},{5,4},{6,7},{7,6},{8,9},{9,8},{10,11... | collective-permute-start | bytes 3145736 | tf_op jit(solution)/shard_map/ppermute | solution.py:274
  75.9 35.2 %all-to-all-start.4 = ((bf16[16,16,2048]{2,1,0:T(8,128)(2,1)}), bf16[16,16,2048]{2,1,0:T(8,128)(2,1)S(1)}, u32[]{:S(2)}, u32[]{:S(2)}) async-start(bf16[16,16,2048]{2,1,0:T(8,128)(2,1)} %fusion), calls=%async_computation.4 | async-start | bytes 2097152 | tf_op jit(solution)/shard_map/all_to_all | solution.py:266
  84.8 0.8 copy-start.7
  111.1 31.5 %all-to-all-start.1 = ((bf16[16,32,1024]{2,1,0:T(8,128)(2,1)}), bf16[16,32,1024]{2,1,0:T(8,128)(2,1)S(1)}, u32[]{:S(2)}, u32[]{:S(2)}) async-start(bf16[16,32,1024]{2,1,0:T(8,128)(2,1)} %copy_bitcast_fusion), calls=%async_computation.1 | async-start | bytes 2097152 | tf_op jit(solution)/shard_map/all_to_all | solution.py:327

commit v2 on v1

--- a/solution.py
+++ b/solution.py
@@ -194,7 +194,7 @@
     back_ref[...] = (back_base_ref[...] + picked[:, width:]).astype(BF16)
 
 
-def on_device(
+def on_device_plain(
     point_feats, region_ids, w_qkv, w_out, w_expert_in, b_expert_in, w_expert_out, out_cotangent
 ):
     wide_count = lax.axis_size("wide")
@@ -338,6 +338,459 @@
     return (layer_out, grad_feats, grad_attention, grad_in, grad_out_w, grad_bias_out)
 
 
+MESH = pl.DeviceIdType.MESH
+
+
+def slot_have(block_len, col, row):
+    points = row.shape[1]
+    first = lax.broadcasted_iota(jnp.int32, (points, points), 0)
+    second = lax.broadcasted_iota(jnp.int32, (points, points), 1)
+    earlier = (col == row) & (first // block_len < second // block_len) & (first % block_len == 0)
+    rank = jnp.sum(earlier.astype(jnp.int32), axis=0, keepdims=True)
+    lane = lax.broadcasted_iota(jnp.int32, (1, points), 1) % block_len
+    return (row * DOMAIN_REPEAT_CAP + rank) * block_len + lane
+
+
+def slot_picks(block_len, experts, expert, rows, have):
+    slot_rows = DOMAIN_REPEAT_CAP * block_len
+    slot = lax.broadcasted_iota(jnp.int32, (rows, 1), 0)
+    region = (slot // (2 * slot_rows)) * experts + expert
+    second = (slot // slot_rows) % 2
+    place = (slot % slot_rows) // block_len
+    want = (region * DOMAIN_REPEAT_CAP + place) * block_len + slot % block_len
+    low = jnp.where(second == 0, want, -1)
+    high = jnp.where(second == 1, want, -1)
+    return [jnp.where(side == have, 1.0, 0.0).astype(BF16) for side in (low, high)]
+
+
+def remote(src, dst, send, recv, device):
+    return pltpu.make_async_remote_copy(
+        src_ref=src, dst_ref=dst, send_sem=send, recv_sem=recv, device_id=device, device_id_type=MESH
+    )
+
+
+def attend_kernel(
+    dims, col_ref, row_ref, x_ref, cot_ref, wqkv_ref, wout_ref,
+    gath_ref, mine_ref, out_ref, back_ref,
+    packed, sums, parts, piece, totals, att, theirs,
+    s_one, r_one, s_two, r_two, s_send, r_send, s_pair, r_pair, s_half, r_half,
+):
+    wide, narrow, experts, block_len, total = dims
+    devices = wide * narrow
+    chunk = 2 * DOMAIN_REPEAT_CAP * block_len
+    here, side = lax.axis_index("wide"), lax.axis_index("narrow")
+    me = here * narrow + side
+    partner = (here, 1 - side)
+    width = x_ref.shape[1]
+    head_dim = width // HEADS
+
+    def peer(k):
+        index = (me + k) % devices
+        return index, (index // narrow, index % narrow)
+
+    barrier = pltpu.get_barrier_semaphore()
+
+    def greet(k, carry):
+        pl.semaphore_signal(barrier, inc=1, device_id=peer(k)[1], device_id_type=MESH)
+        return carry
+
+    lax.fori_loop(1, devices, greet, 0)
+
+    mask = head_mask(width, head_dim)
+    mean_mat = jnp.where(mask, 1.0 / head_dim, 0.0).astype(BF16)
+
+    def normalize(raw):
+        centred = raw.astype(F32) - dot(raw, mean_mat)
+        scale = jnp.sqrt(dot_split(centred * centred, mean_mat) + 1e-05)
+        return centred / scale, scale
+
+    def fold(full):
+        kept = jnp.where(mask, full, 0.0) * (1.0 / total)
+        return jnp.sum(kept.reshape(HEADS, head_dim, width), axis=0)
+
+    x, cot = x_ref[...], cot_ref[...]
+    q = dot(x, wqkv_ref[:, :width]).astype(BF16)
+    k_unit, k_scale = normalize(dot(x, wqkv_ref[:, width : 2 * width]).astype(BF16))
+    v_unit, v_scale = normalize(dot(x, wqkv_ref[:, 2 * width :]).astype(BF16))
+    grad_mixed = dot(cot, wout_ref[...], 1, 1).astype(BF16)
+    k_norm, v_norm = k_unit.astype(BF16), v_unit.astype(BF16)
+    both = jnp.concatenate([fold(dot(k_norm, v_norm, 0, 0)), fold(dot(q, grad_mixed, 0, 0))], axis=0)
+    tall = jnp.concatenate([both[:, p * 128 : (p + 1) * 128] for p in range(width // 128)], axis=0)
+    sums[...] = tall.reshape(sums.shape)
+    pl.semaphore_wait(barrier, devices - 1)
+
+    def one(k):
+        index, device = peer(k)
+        return remote(sums.at[index], parts.at[k], s_one.at[k], r_one.at[k], device)
+
+    def two(k):
+        return remote(piece, totals.at[me], s_two.at[k], r_two.at[k], peer(k)[1])
+
+    def span(index):
+        return pl.ds(pl.multiple_of(index * chunk, chunk), chunk)
+
+    def send(k):
+        dest = (here + k) % wide
+        return remote(
+            packed.at[span(dest)], gath_ref.at[span(here)], s_send.at[k], r_send.at[k], (dest, side)
+        )
+
+    def forward(k):
+        source = (here - k + wide) % wide
+        return remote(
+            gath_ref.at[span(source)], gath_ref.at[span(wide + source)],
+            s_pair.at[k], r_pair.at[k], partner,
+        )
+
+    def each(low, high, action):
+        def body(k, carry):
+            action(k)
+            return carry
+
+        lax.fori_loop(low, high, body, 0)
+
+    each(1, devices, lambda k: one(k).start())
+    parts[0] = sums[me]
+    have = slot_have(block_len, col_ref[...], row_ref[...])
+    for expert in range(experts):
+        first, second = slot_picks(block_len, experts, expert, packed.shape[0], have)
+        packed[:, expert * width : (expert + 1) * width] = (dot(first, x) + dot(second, cot)).astype(BF16)
+    each(1, devices, lambda k: one(k).wait_recv())
+    whole = jnp.sum(parts[...], axis=0)
+    piece[...] = whole
+    totals[me] = whole
+    each(1, devices, lambda k: two(k).start())
+    each(1, wide, lambda k: send(k).start())
+    gath_ref[span(here), :] = packed[span(here), :]
+    forward(0).start()
+    each(1, devices, lambda k: two(k).wait_recv())
+
+    tall = totals[...].reshape(devices * totals.shape[1], 128)
+    step = tall.shape[0] // (width // 128)
+    both = jnp.concatenate([tall[p * step : (p + 1) * step] for p in range(width // 128)], axis=1)
+
+    def spread(folded):
+        return jnp.where(mask, jnp.concatenate([folded] * HEADS, axis=0), 0.0).astype(BF16)
+
+    summary, grad_summary = spread(both[:head_dim]), spread(both[head_dim:])
+
+    def back(grad, unit, scale):
+        mean_grad = dot_split(grad, mean_mat)
+        mean_cross = dot_split(grad * unit, mean_mat)
+        return ((grad - mean_grad - unit * mean_cross) / scale).astype(BF16)
+
+    mixed = dot(q, summary).astype(BF16)
+    grad_query = dot(grad_mixed, summary, 1, 1).astype(BF16)
+    grad_key = back(dot(v_norm, grad_summary, 1, 1), k_unit, k_scale)
+    grad_value = back(dot(k_norm, grad_summary), v_unit, v_scale)
+    x_turned = x.T
+    mixed_turned = mixed.T
+    for block, (left, right) in enumerate(
+        [(x_turned, grad_query), (x_turned, grad_key), (x_turned, grad_value), (mixed_turned, cot)]
+    ):
+        value = (dot(left, right) * (1.0 / total)).reshape(wide, narrow, -1, width)
+        for part in range(narrow):
+            att[part, :, :, block * width : (block + 1) * width] = value[:, part].astype(BF16)
+    swap = remote(att.at[1 - side], theirs, s_half, r_half, partner)
+    swap.start()
+    out_ref[...] = x.astype(F32) + dot(mixed, wout_ref[...])
+    back_ref[...] = (
+        cot.astype(F32)
+        + dot(grad_query, wqkv_ref[:, :width], 1, 1)
+        + dot(grad_key, wqkv_ref[:, width : 2 * width], 1, 1)
+        + dot(grad_value, wqkv_ref[:, 2 * width :], 1, 1)
+    )
+    swap.wait()
+    mine_ref[...] = (att[side].astype(F32) + theirs[...].astype(F32)).astype(BF16)
+
+    def pass_on(k):
+        send(k).wait_recv()
+        forward(k).start()
+
+    each(1, wide, pass_on)
+    each(0, wide, lambda k: forward(k).wait_recv())
+    each(0, wide, lambda k: forward(k).wait_send())
+    each(1, wide, lambda k: send(k).wait_send())
+    each(1, devices, lambda k: one(k).wait_send())
+    each(1, devices, lambda k: two(k).wait_send())
+
+
+def split_rows(block, slot_rows):
+    rows, width = block.shape
+    floats = block.astype(F32).reshape(rows // (2 * slot_rows), 2, slot_rows, width)
+    return [floats[:, i].reshape(rows // 2, width).astype(BF16) for i in range(2)]
+
+
+def region_kernel(
+    dims, gath_ref, win_ref, bias_ref, wout_ref, mine_ref, col_ref, row_ref, out_base_ref, back_base_ref,
+    hidden_ref, gpre_ref, out_ref, back_ref, gatt_ref,
+    feats, cots, out_acc, back_acc, ret_send, ret_recv, stage_one, stage_sum, stage_two,
+    s_ret, r_ret, s_one, r_one, s_two, r_two,
+):
+    wide, plane, experts, block_len = dims
+    levels = wide // plane
+    slot_rows = DOMAIN_REPEAT_CAP * block_len
+    chunk = 2 * slot_rows
+    here, side = lax.axis_index("wide"), lax.axis_index("narrow")
+    level, spot = here // plane, here % plane
+    expert, step = pl.program_id(0), pl.program_id(1)
+    last_step = pl.num_programs(1) - 1
+    own, width = out_acc.shape
+
+    def each(low, high, action):
+        def body(k, carry):
+            action(k)
+            return carry
+
+        lax.fori_loop(low, high, body, 0)
+
+    def span(index):
+        return pl.ds(pl.multiple_of(index * chunk, chunk), chunk)
+
+    def give(e, k):
+        dest = (here + k) % wide
+        return remote(
+            ret_send.at[e, span(dest)], ret_recv.at[e, span(here)],
+            s_ret.at[e, k], r_ret.at[e, k], (dest, side),
+        )
+
+    def one(k):
+        other = (spot + k) % plane
+        return remote(
+            mine_ref.at[:, other], stage_one.at[k], s_one.at[k], r_one.at[k],
+            (level * plane + other, side),
+        )
+
+    def two(k):
+        other = (level + k) % levels
+        return remote(
+            stage_sum.at[other], stage_two.at[k], s_two.at[k], r_two.at[k],
+            (other * plane + spot, side),
+        )
+
+    @pl.when((expert == 0) & (step == 0))
+    def _():
+        barrier = pltpu.get_barrier_semaphore()
+        each(
+            1, wide,
+            lambda k: pl.semaphore_signal(
+                barrier, inc=1, device_id=((here + k) % wide, side), device_id_type=MESH
+            ),
+        )
+        pl.semaphore_wait(barrier, wide - 1)
+        each(1, plane, lambda k: one(k).start())
+        stage_one[0] = mine_ref[:, spot]
+
+    @pl.when((expert == 1) & (step == 0))
+    def _():
+        each(1, plane, lambda k: one(k).wait())
+        summed = jnp.sum(stage_one[...].astype(F32), axis=0).astype(BF16)
+        stage_sum[...] = summed
+        each(1, levels, lambda k: two(k).start())
+        stage_two[0] = stage_sum[level]
+
+    @pl.when(step == 0)
+    def _():
+        feats[...], cots[...] = split_rows(gath_ref[...], slot_rows)
+
+    w_in, w_out = win_ref[...], wout_ref[...]
+    pre = dot(feats[...], w_in) + bias_ref[...]
+    grad_hidden = dot(cots[...], w_out, 1, 1)
+    square = pre * pre
+    tangent = jnp.tanh(gelu_scale * (pre + gelu_cubic * square * pre))
+    half_sum = 0.5 * (1.0 + tangent)
+    hidden = (pre * half_sum).astype(BF16)
+    slope = half_sum + 0.5 * pre * (1.0 - tangent * tangent) * gelu_scale * (1.0 + 3.0 * gelu_cubic * square)
+    grad_pre = (grad_hidden * slope).astype(BF16)
+    hidden_ref[...] = hidden
+    gpre_ref[...] = grad_pre
+    out_part = dot(hidden[:own], w_out)
+    back_part = dot(grad_pre[:own], w_in, 1, 1)
+
+    @pl.when(step == 0)
+    def _():
+        out_acc[...] = out_part
+        back_acc[...] = back_part
+
+    @pl.when(step > 0)
+    def _():
+        out_acc[...] += out_part
+        back_acc[...] += back_part
+
+    @pl.when(step == last_step)
+    def _():
+        pair = jnp.concatenate(
+            [ref[...].reshape(wide, slot_rows, width) for ref in (out_acc, back_acc)], axis=1
+        )
+        ret_send[expert] = pair.reshape(wide * chunk, width).astype(BF16)
+        each(1, wide, lambda k: give(expert, k).start())
+        ret_recv[expert, span(here), :] = ret_send[expert, span(here), :]
+
+    @pl.when((expert == experts - 1) & (step == last_step))
+    def _():
+        each(1, levels, lambda k: two(k).wait())
+        gatt_ref[...] = jnp.sum(stage_two[...].astype(F32), axis=0)
+        have = slot_have(block_len, col_ref[...], row_ref[...])
+        out, back = out_base_ref[...], back_base_ref[...]
+        for e in range(experts):
+            each(1, wide, lambda k: give(e, k).wait_recv())
+            first, second = slot_picks(block_len, experts, e, wide * chunk, have)
+            rows = ret_recv[e]
+            out += dot(first, rows, 0, 0)
+            back += dot(second, rows, 0, 0)
+        out_ref[...] = out.astype(BF16)
+        back_ref[...] = back.astype(BF16)
+        for e in range(experts):
+            each(1, wide, lambda k: give(e, k).wait_send())
+
+
+def weight_kernel(
+    share, slot_rows, half_ref, gath_feat_ref, hidden_ref, gpre_ref, gin_ref, gout_ref, gbias_ref, feats, cots
+):
+    @pl.when(pl.program_id(1) == 0)
+    def _():
+        feat, cot = split_rows(gath_feat_ref[...], slot_rows)
+        feats[...] = feat.T
+        cots[...] = cot
+
+    grad_pre = gpre_ref[...]
+    gin_ref[...] = dot(feats[...], grad_pre) * share
+    gout_ref[...] = dot(hidden_ref[...], cots[...], 0, 0) * share
+    gbias_ref[...] = jnp.sum(grad_pre.astype(F32), axis=0, keepdims=True) * share
+
+
+def on_device(
+    point_feats, region_ids, w_qkv, w_out, w_expert_in, b_expert_in, w_expert_out, out_cotangent
+):
+    wide = lax.axis_size("wide")
+    narrow = lax.axis_size("narrow")
+    devices = wide * narrow
+    points, width = point_feats.shape
+    total = points * devices
+    block_len = points // region_ids.shape[0]
+    slab = w_expert_in.shape[1]
+    experts = DOMAIN_SPECIALS // wide
+    plane = 4
+    if narrow != 2 or experts < 2 or wide % plane or width % (16 * devices):
+        return on_device_plain(
+            point_feats, region_ids, w_qkv, w_out, w_expert_in, b_expert_in, w_expert_out, out_cotangent
+        )
+    hid = slab // experts
+    slot_rows = DOMAIN_REPEAT_CAP * block_len
+    chunk = 2 * slot_rows
+    fold_rows = 2 * (width // HEADS) * (width // 128) // devices
+    share_rows = width // devices
+    labels = jnp.repeat(region_ids, block_len)
+    col, row = labels[:, None], labels[None, :]
+    wide_bf = jax.ShapeDtypeStruct((points, width), BF16)
+    wide_f = jax.ShapeDtypeStruct((points, width), F32)
+    dma = pltpu.SemaphoreType.DMA
+
+    def remote_params(identity):
+        return pltpu.CompilerParams(
+            collective_id=identity, has_side_effects=True, vmem_limit_bytes=48 * 2**20
+        )
+
+    gathered, mine, out_base, back_base = pl.pallas_call(
+        functools.partial(attend_kernel, (wide, narrow, experts, block_len, total)),
+        out_shape=(
+            jax.ShapeDtypeStruct((narrow * wide * chunk, experts * width), BF16),
+            jax.ShapeDtypeStruct((wide, share_rows, 4 * width), BF16),
+            wide_f, wide_f,
+        ),
+        in_specs=[VMEM_SPEC] * 6,
+        out_specs=[VMEM_SPEC] * 4,
+        scratch_shapes=[
+            pltpu.VMEM((wide * chunk, experts * width), BF16),
+            pltpu.VMEM((devices, fold_rows, 128), F32),
+            pltpu.VMEM((devices, fold_rows, 128), F32),
+            pltpu.VMEM((fold_rows, 128), F32),
+            pltpu.VMEM((devices, fold_rows, 128), F32),
+            pltpu.VMEM((narrow, wide, share_rows, 4 * width), BF16),
+            pltpu.VMEM((wide, share_rows, 4 * width), BF16),
+            dma((devices,)), dma((devices,)), dma((devices,)), dma((devices,)),
+            dma((wide,)), dma((wide,)), dma((wide,)), dma((wide,)), dma, dma,
+        ],
+        compiler_params=remote_params(0),
+        name="attend",
+    )(col, row, point_feats, out_cotangent, w_qkv, w_out)
+
+    own = wide * slot_rows
+    all_rows = own * narrow
+    tile = min(512, hid)
+    steps = hid // tile
+    levels = wide // plane
+    slab_bf = jax.ShapeDtypeStruct((all_rows, slab), BF16)
+    hidden, grad_pre, layer_out, grad_feats, grad_attention = pl.pallas_call(
+        functools.partial(region_kernel, (wide, plane, experts, block_len)),
+        out_shape=(
+            slab_bf, slab_bf, wide_bf, wide_bf, jax.ShapeDtypeStruct((share_rows, 4 * width), F32),
+        ),
+        grid=(experts, steps),
+        in_specs=[
+            pl.BlockSpec((narrow * wide * chunk, width), lambda e, t: (0, e)),
+            pl.BlockSpec((width, tile), lambda e, t: (0, e * steps + t)),
+            pl.BlockSpec((1, tile), lambda e, t: (0, e * steps + t)),
+            pl.BlockSpec((tile, width), lambda e, t: (e * steps + t, 0)),
+        ] + [VMEM_SPEC] * 5,
+        out_specs=[
+            pl.BlockSpec((all_rows, tile), lambda e, t: (0, e * steps + t)),
+            pl.BlockSpec((all_rows, tile), lambda e, t: (0, e * steps + t)),
+        ] + [VMEM_SPEC] * 3,
+        scratch_shapes=[
+            pltpu.VMEM((all_rows, width), BF16),
+            pltpu.VMEM((all_rows, width), BF16),
+            pltpu.VMEM((own, width), F32),
+            pltpu.VMEM((own, width), F32),
+            pltpu.VMEM((experts, wide * chunk, width), BF16),
+            pltpu.VMEM((experts, wide * chunk, width), BF16),
+            pltpu.VMEM((plane, levels, share_rows, 4 * width), BF16),
+            pltpu.VMEM((levels, share_rows, 4 * width), BF16),
+            pltpu.VMEM((levels, share_rows, 4 * width), BF16),
+            dma((experts, wide)), dma((experts, wide)),
+            dma((plane,)), dma((plane,)), dma((levels,)), dma((levels,)),
+        ],
+        compiler_params=remote_params(1),
+        name="regions",
+    )(
+        gathered, w_expert_in, b_expert_in[None, :], w_expert_out,
+        mine.reshape(levels, plane, share_rows, 4 * width), col, row, out_base, back_base,
+    )
+
+    half = width // narrow
+    side = lax.axis_index("narrow")
+    wtile = min(1024, hid)
+    wsteps = hid // wtile
+    grad_in, grad_out_w, grad_bias = pl.pallas_call(
+        functools.partial(weight_kernel, DOMAIN_SPECIALS / total, slot_rows),
+        out_shape=(
+            jax.ShapeDtypeStruct((half, slab), F32),
+            jax.ShapeDtypeStruct((slab, half), F32),
+            jax.ShapeDtypeStruct((1, slab), F32),
+        ),
+        grid_spec=pltpu.PrefetchScalarGridSpec(
+            num_scalar_prefetch=1,
+            grid=(experts, wsteps),
+            in_specs=[
+                pl.BlockSpec((narrow * wide * chunk, half), lambda e, t, n: (0, e * narrow + n[0])),
+                pl.BlockSpec((all_rows, wtile), lambda e, t, n: (0, e * wsteps + t)),
+                pl.BlockSpec((all_rows, wtile), lambda e, t, n: (0, e * wsteps + t)),
+            ],
+            out_specs=[
+                pl.BlockSpec((half, wtile), lambda e, t, n: (0, e * wsteps + t)),
+                pl.BlockSpec((wtile, half), lambda e, t, n: (e * wsteps + t, 0)),
+                pl.BlockSpec((1, wtile), lambda e, t, n: (0, e * wsteps + t)),
+            ],
+            scratch_shapes=[pltpu.VMEM((half, all_rows), BF16), pltpu.VMEM((all_rows, half), BF16)],
+        ),
+        name="weights",
+        **params(8 * all_rows * half * slab, 8 * width * slab),
+    )(side.astype(jnp.int32)[None], gathered, hidden, grad_pre)
+    bias_half = slab // narrow
+    grad_bias_out = lax.dynamic_slice_in_dim(grad_bias[0], side * bias_half, bias_half, 0)
+    return (layer_out, grad_feats, grad_attention, grad_in, grad_out_w, grad_bias_out)
+
+
 def solution(mesh):
     placed = (
         P(("wide", "narrow"), None),

time: 145 us -> 120 us (0.83)
  Pallas kernels: 34.9 us -> 108 us
  waiting for transfers between devices: 41.8 us -> 0 us
  starting transfers between devices: 20.1 us -> 0 us
  blocking collectives: 17.7 us -> 0 us
  local copies, waits for them, and re-layouts: 24.8 us -> 10.3 us
  other arithmetic: 3.61 us -> 0 us
    pallas_call x5 -> x3, Pallas kernels: 34.9 us -> 108 us  [the longest x1 54.6 us: on_device(): pl.pallas_call(functools.partial(region_kernel, (wide, plane, experts, bl...]
    all_to_all x4 -> x0, waiting for transfers between devices: 41.8 us -> none  [the longest x1 23.1 us: on_device(): lax.all_to_all(returned, 'wide', split_axis=0, concat_axis=0, tiled=True)]
    all_to_all x4 -> x0, starting transfers between devices: 20.1 us -> none  [the longest x1 6.91 us: on_device(): lax.all_to_all(returned, 'wide', split_axis=0, concat_axis=0, tiled=True)]
    all_to_all x1 -> x0, blocking collectives: 17.7 us -> none  [on_device(): pieces = lax.all_to_all(sums, axes, split_axis=0, concat_axis=0, tiled=True)]
    unnamed x48 -> x17, local copies, waits for them, and re-layouts: 17.1 us -> 8.75 us
    convert_element_type x1 -> x0, other arithmetic: 2.6 us -> none  [on_device(): mine.astype(BF16).reshape(wide_count * (width // device_count), 4 * width)]
    squeeze x1 -> x0, local copies, waits for them, and re-layouts: 2.47 us -> none  [on_device(): theirs = lax.dynamic_index_in_dim(att, other, 1, keepdims=False)]
  transfers between devices with their start and end apart: 6 -> 0, of which waited for: 3 -> 0; matrix products, arithmetic and copies ran while one was open for 7% -> 0% of each run, Pallas kernels for 22% -> 0%
where the time goes in v2:
time: 120 us; the launch traced here: 119 us
  Pallas kernels  108 us (90%)
  local copies, waits for them, and re-layouts  10.3 us (9%)
    pallas_call x1, Pallas kernels, on_device(): pl.pallas_call(functools.partial(region_kernel, (wide, plane, experts, bl...  54.6 us
    pallas_call x1, Pallas kernels, on_device(): pl.pallas_call(functools.partial(attend_kernel, (wide, narrow, experts, b...  42 us
    pallas_call x1, Pallas kernels, on_device(): pl.pallas_call(functools.partial(weight_kernel, DOMAIN_SPECIALS / total,...  11.7 us
    unnamed x17, local copies, waits for them, and re-layouts  8.75 us

profile of v2, /device:TPU:0, one launch (start us, length us, event | category | flops | bytes accessed | tf_op | source)
XLA Modules:
  0.0 119.3 jit_solution(14726773528631593385)
XLA Ops:
  0.6 0.7 broadcast_in_dim.9
  1.4 0.1 broadcast_in_dim_reshape.8.col_ref
  1.5 0.1 broadcast_in_dim_reshape.7.row_ref
  1.6 0.0 copy-start.2
  1.6 1.4 %copy-done.2 = bf16[512,1536]{1,0:T(8,128)(2,1)S(1)} copy-done((bf16[512,1536]{1,0:T(8,128)(2,1)S(1)}, bf16[512,1536]{1,0:T(8,128)(2,1)}, u32[]{:S(2)}) %copy-start.2) | copy-done | bytes 1572888
  3.0 0.0 copy-start.3
  3.0 1.0 copy-done.3
  4.0 0.0 copy-start.4
  4.0 0.9 copy-done.4
  5.0 0.0 copy-start.5
  5.0 0.9 copy-done.5
  5.9 42.0 %attend.1 = (bf16[512,2048]{1,0:T(8,128)(2,1)}, bf16[16,16,2048]{2,1,0:T(8,128)(2,1)S(1)}, f32[256,512]{1,0:T(8,128)S(1)}, f32[256,512]{1,0:T(8,128)S(1)}) custom-call(s32[256,1]{1,0:T(8,128)S(1)} %broadcast_in_dim_reshape.8.col_ref, s32[1,256]{1,0:T(1,128)S(1)} %broadcast_in_dim_reshape.7.row_ref, bf16[256,512]{1,0:T(8,128)(2,1)S(1)} %copy-done.4, ...), custom_call_target="tpu_custom_call" | custom-call | tf_op jit(solution)/shard_map/attend/pallas_call | solution.py:694
  47.9 0.0 copy-start
  47.9 1.6 %copy-done = bf16[512,2048]{1,0:T(8,128)(2,1)S(1)} copy-done((bf16[512,2048]{1,0:T(8,128)(2,1)S(1)}, bf16[512,2048]{1,0:T(8,128)(2,1)}, u32[]{:S(2)}) %copy-start) | copy-done | bytes 2097176
  49.5 0.0 copy-start.6
  49.5 0.8 copy-done.6
  50.3 0.0 copy-start.1
  50.3 54.6 %regions.1 = (bf16[256,8192]{1,0:T(8,128)(2,1)}, bf16[256,8192]{1,0:T(8,128)(2,1)}, bf16[256,512]{1,0:T(8,128)(2,1)S(1)}, bf16[256,512]{1,0:T(8,128)(2,1)S(1)}, f32[16,2048]{1,0:T(8,128)S(1)}) custom-call(bf16[512,2048]{1,0:T(8,128)(2,1)S(1)} %copy-done, bf16[512,8192]{1,0:T(8,128)(2,1)} %win_ref.1, f32[1,8192]{1,0:T(1,128)S(1)} %bitcast.5, ...), custom_call_target="tpu_custom_call" | custom-call | tf_op jit(solution)/shard_map/regions/pallas_call | solution.py:724
  104.9 0.0 copy-done.1
  104.9 11.7 %weights.1 = (f32[256,8192]{1,0:T(8,128)}, f32[8192,256]{1,0:T(8,128)}, f32[1,8192]{1,0:T(1,128)S(1)}) custom-call(s32[1]{0:T(128)} %bitcast.2.half_ref, bf16[512,2048]{1,0:T(8,128)(2,1)S(1)} %copy-done.1, bf16[256,8192]{1,0:T(8,128)(2,1)} %get-tuple-element.25.hidden_ref, bf16[256,8192]{1,0:T(8,128)(2,1)} %get-tuple-element.26.gpre_ref), custom_call_target="tpu_custom_call" | custom-call | flops 4294967296 | bytes 33554432 | tf_op jit(solution)/shard_map/weights/pallas_call | solution.py:764
  116.6 0.6 constant_dynamic-slice_fusion
  117.2 0.7 copy.19
  117.9 0.7 copy.20
  118.6 0.7 copy.21
Async XLA Ops:
  1.6 1.4 %copy-start.2 = (bf16[512,1536]{1,0:T(8,128)(2,1)S(1)}, bf16[512,1536]{1,0:T(8,128)(2,1)}, u32[]{:S(2)}) copy-start(bf16[512,1536]{1,0:T(8,128)(2,1)} %wqkv_ref.1) | copy-start | bytes 4718596
  3.0 1.0 copy-start.3
  4.0 0.9 copy-start.4
  5.0 0.9 copy-start.5
  47.9 1.6 %copy-start = (bf16[512,2048]{1,0:T(8,128)(2,1)S(1)}, bf16[512,2048]{1,0:T(8,128)(2,1)}, u32[]{:S(2)}) copy-start(bf16[512,2048]{1,0:T(8,128)(2,1)} %get-tuple-element.18.gath_ref.gath_feat_ref) | copy-start | bytes 6291460
  49.5 0.8 copy-start.6
  50.3 54.6 %copy-start.1 = (bf16[512,2048]{1,0:T(8,128)(2,1)S(1)}, bf16[512,2048]{1,0:T(8,128)(2,1)}, u32[]{:S(2)}) copy-start(bf16[512,2048]{1,0:T(8,128)(2,1)} %get-tuple-element.18.gath_ref.gath_feat_ref) | copy-start | bytes 6291460

commit v3 on v2

--- a/solution.py
+++ b/solution.py
@@ -18,6 +18,7 @@
 F32 = jnp.float32
 BF16 = jnp.bfloat16
 VMEM_SPEC = pl.BlockSpec(memory_space=pltpu.VMEM)
+HBM_SPEC = pl.BlockSpec(memory_space=pltpu.HBM)
 
 
 def dot(a, b, ca=1, cb=0):
@@ -370,10 +371,10 @@
 
 
 def attend_kernel(
-    dims, col_ref, row_ref, x_ref, cot_ref, wqkv_ref, wout_ref,
+    dims, col_ref, row_ref, x_hbm, cot_hbm, wqkv_hbm, wout_hbm,
     gath_ref, mine_ref, out_ref, back_ref,
-    packed, sums, parts, piece, totals, att, theirs,
-    s_one, r_one, s_two, r_two, s_send, r_send, s_pair, r_pair, s_half, r_half,
+    x_ref, cot_ref, wqkv_ref, wout_ref, packed, sums, parts, piece, totals, att, theirs,
+    s_one, r_one, s_two, r_two, s_send, r_send, s_pair, r_pair, s_half, r_half, s_in, s_own,
 ):
     wide, narrow, experts, block_len, total = dims
     devices = wide * narrow
@@ -388,6 +389,10 @@
         index = (me + k) % devices
         return index, (index // narrow, index % narrow)
 
+    sources = [(x_hbm, x_ref), (cot_hbm, cot_ref), (wqkv_hbm, wqkv_ref), (wout_hbm, wout_ref)]
+    loads = [pltpu.make_async_copy(a, b, s_in.at[i]) for i, (a, b) in enumerate(sources)]
+    for load in loads:
+        load.start()
     barrier = pltpu.get_barrier_semaphore()
 
     def greet(k, carry):
@@ -408,7 +413,15 @@
         kept = jnp.where(mask, full, 0.0) * (1.0 / total)
         return jnp.sum(kept.reshape(HEADS, head_dim, width), axis=0)
 
+    loads[0].wait()
+    loads[1].wait()
     x, cot = x_ref[...], cot_ref[...]
+    have = slot_have(block_len, col_ref[...], row_ref[...])
+    for expert in range(experts):
+        first, second = slot_picks(block_len, experts, expert, packed.shape[0], have)
+        packed[:, expert * width : (expert + 1) * width] = (dot(first, x) + dot(second, cot)).astype(BF16)
+    loads[2].wait()
+    loads[3].wait()
     q = dot(x, wqkv_ref[:, :width]).astype(BF16)
     k_unit, k_scale = normalize(dot(x, wqkv_ref[:, width : 2 * width]).astype(BF16))
     v_unit, v_scale = normalize(dot(x, wqkv_ref[:, 2 * width :]).astype(BF16))
@@ -435,10 +448,10 @@
             packed.at[span(dest)], gath_ref.at[span(here)], s_send.at[k], r_send.at[k], (dest, side)
         )
 
-    def forward(k):
+    def forward(held, k):
         source = (here - k + wide) % wide
         return remote(
-            gath_ref.at[span(source)], gath_ref.at[span(wide + source)],
+            held.at[span(source)], gath_ref.at[span(wide + source)],
             s_pair.at[k], r_pair.at[k], partner,
         )
 
@@ -451,18 +464,16 @@
 
     each(1, devices, lambda k: one(k).start())
     parts[0] = sums[me]
-    have = slot_have(block_len, col_ref[...], row_ref[...])
-    for expert in range(experts):
-        first, second = slot_picks(block_len, experts, expert, packed.shape[0], have)
-        packed[:, expert * width : (expert + 1) * width] = (dot(first, x) + dot(second, cot)).astype(BF16)
+    each(1, wide // 2, lambda k: send(k).start())
+    keep = pltpu.make_async_copy(packed.at[span(here)], gath_ref.at[span(here)], s_own)
+    keep.start()
+    forward(packed, 0).start()
     each(1, devices, lambda k: one(k).wait_recv())
     whole = jnp.sum(parts[...], axis=0)
     piece[...] = whole
     totals[me] = whole
     each(1, devices, lambda k: two(k).start())
-    each(1, wide, lambda k: send(k).start())
-    gath_ref[span(here), :] = packed[span(here), :]
-    forward(0).start()
+    each(wide // 2, wide, lambda k: send(k).start())
     each(1, devices, lambda k: two(k).wait_recv())
 
     tall = totals[...].reshape(devices * totals.shape[1], 128)
@@ -505,11 +516,12 @@
 
     def pass_on(k):
         send(k).wait_recv()
-        forward(k).start()
+        forward(gath_ref, k).start()
 
     each(1, wide, pass_on)
-    each(0, wide, lambda k: forward(k).wait_recv())
-    each(0, wide, lambda k: forward(k).wait_send())
+    keep.wait()
+    forward(packed, 0).wait()
+    each(1, wide, lambda k: forward(gath_ref, k).wait())
     each(1, wide, lambda k: send(k).wait_send())
     each(1, devices, lambda k: one(k).wait_send())
     each(1, devices, lambda k: two(k).wait_send())
@@ -522,13 +534,14 @@
 
 
 def region_kernel(
-    dims, gath_ref, win_ref, bias_ref, wout_ref, mine_ref, col_ref, row_ref, out_base_ref, back_base_ref,
-    hidden_ref, gpre_ref, out_ref, back_ref, gatt_ref,
+    dims, gath_ref, win_ref, bias_ref, wout_ref, mine_ref,
+    hidden_ref, gpre_ref, first_ref, late_ref, gatt_ref,
     feats, cots, out_acc, back_acc, ret_send, ret_recv, stage_one, stage_sum, stage_two,
     s_ret, r_ret, s_one, r_one, s_two, r_two,
 ):
     wide, plane, experts, block_len = dims
     levels = wide // plane
+    early = ret_send.shape[0]
     slot_rows = DOMAIN_REPEAT_CAP * block_len
     chunk = 2 * slot_rows
     here, side = lax.axis_index("wide"), lax.axis_index("narrow")
@@ -622,26 +635,45 @@
         pair = jnp.concatenate(
             [ref[...].reshape(wide, slot_rows, width) for ref in (out_acc, back_acc)], axis=1
         )
-        ret_send[expert] = pair.reshape(wide * chunk, width).astype(BF16)
-        each(1, wide, lambda k: give(expert, k).start())
-        ret_recv[expert, span(here), :] = ret_send[expert, span(here), :]
+        pair = pair.astype(BF16)
+
+        @pl.when(expert < early)
+        def _():
+            ret_send[expert] = pair.reshape(wide * chunk, width)
+            each(1, wide, lambda k: give(expert, k).start())
+            ret_recv[expert, span(here), :] = ret_send[expert, span(here), :]
+
+        @pl.when(expert >= early)
+        def _():
+            late_ref[:, expert - early] = pair
 
     @pl.when((expert == experts - 1) & (step == last_step))
     def _():
         each(1, levels, lambda k: two(k).wait())
         gatt_ref[...] = jnp.sum(stage_two[...].astype(F32), axis=0)
-        have = slot_have(block_len, col_ref[...], row_ref[...])
-        out, back = out_base_ref[...], back_base_ref[...]
-        for e in range(experts):
-            each(1, wide, lambda k: give(e, k).wait_recv())
-            first, second = slot_picks(block_len, experts, e, wide * chunk, have)
-            rows = ret_recv[e]
-            out += dot(first, rows, 0, 0)
-            back += dot(second, rows, 0, 0)
-        out_ref[...] = out.astype(BF16)
-        back_ref[...] = back.astype(BF16)
-        for e in range(experts):
-            each(1, wide, lambda k: give(e, k).wait_send())
+        for e in range(early):
+            each(1, wide, lambda k: give(e, k).wait())
+            first_ref[e] = ret_recv[e]
+
+
+def sum_kernel(
+    block_len, experts, col_ref, row_ref, first_ref, late_ref, out_base_ref, back_base_ref, out_ref, back_ref
+):
+    early = first_ref.shape[0]
+    rows = first_ref.shape[1]
+    width = out_ref.shape[1]
+    have = slot_have(block_len, col_ref[...], row_ref[...])
+    out, back = out_base_ref[...], back_base_ref[...]
+    for e in range(experts):
+        first, second = slot_picks(block_len, experts, e, rows, have)
+        if e < early:
+            data = first_ref[e]
+        else:
+            data = late_ref[:, e - early].reshape(rows, width)
+        out += dot(first, data, 0, 0)
+        back += dot(second, data, 0, 0)
+    out_ref[...] = out.astype(BF16)
+    back_ref[...] = back.astype(BF16)
 
 
 def weight_kernel(
@@ -686,9 +718,9 @@
     wide_f = jax.ShapeDtypeStruct((points, width), F32)
     dma = pltpu.SemaphoreType.DMA
 
-    def remote_params(identity):
+    def remote_params(identity, vmem):
         return pltpu.CompilerParams(
-            collective_id=identity, has_side_effects=True, vmem_limit_bytes=48 * 2**20
+            collective_id=identity, has_side_effects=True, vmem_limit_bytes=vmem * 2**20
         )
 
     gathered, mine, out_base, back_base = pl.pallas_call(
@@ -698,9 +730,13 @@
             jax.ShapeDtypeStruct((wide, share_rows, 4 * width), BF16),
             wide_f, wide_f,
         ),
-        in_specs=[VMEM_SPEC] * 6,
-        out_specs=[VMEM_SPEC] * 4,
+        in_specs=[VMEM_SPEC] * 2 + [HBM_SPEC] * 4,
+        out_specs=[HBM_SPEC] + [VMEM_SPEC] * 3,
         scratch_shapes=[
+            pltpu.VMEM(point_feats.shape, BF16),
+            pltpu.VMEM(out_cotangent.shape, BF16),
+            pltpu.VMEM(w_qkv.shape, BF16),
+            pltpu.VMEM(w_out.shape, BF16),
             pltpu.VMEM((wide * chunk, experts * width), BF16),
             pltpu.VMEM((devices, fold_rows, 128), F32),
             pltpu.VMEM((devices, fold_rows, 128), F32),
@@ -709,9 +745,9 @@
             pltpu.VMEM((narrow, wide, share_rows, 4 * width), BF16),
             pltpu.VMEM((wide, share_rows, 4 * width), BF16),
             dma((devices,)), dma((devices,)), dma((devices,)), dma((devices,)),
-            dma((wide,)), dma((wide,)), dma((wide,)), dma((wide,)), dma, dma,
+            dma((wide,)), dma((wide,)), dma((wide,)), dma((wide,)), dma, dma, dma((4,)), dma,
         ],
-        compiler_params=remote_params(0),
+        compiler_params=remote_params(0, 60),
         name="attend",
     )(col, row, point_feats, out_cotangent, w_qkv, w_out)
 
@@ -721,10 +757,14 @@
     steps = hid // tile
     levels = wide // plane
     slab_bf = jax.ShapeDtypeStruct((all_rows, slab), BF16)
-    hidden, grad_pre, layer_out, grad_feats, grad_attention = pl.pallas_call(
+    early = experts // 2
+    hidden, grad_pre, ret_first, ret_late, grad_attention = pl.pallas_call(
         functools.partial(region_kernel, (wide, plane, experts, block_len)),
         out_shape=(
-            slab_bf, slab_bf, wide_bf, wide_bf, jax.ShapeDtypeStruct((share_rows, 4 * width), F32),
+            slab_bf, slab_bf,
+            jax.ShapeDtypeStruct((early, wide * chunk, width), BF16),
+            jax.ShapeDtypeStruct((wide, experts - early, chunk, width), BF16),
+            jax.ShapeDtypeStruct((share_rows, 4 * width), F32),
         ),
         grid=(experts, steps),
         in_specs=[
@@ -732,7 +772,7 @@
             pl.BlockSpec((width, tile), lambda e, t: (0, e * steps + t)),
             pl.BlockSpec((1, tile), lambda e, t: (0, e * steps + t)),
             pl.BlockSpec((tile, width), lambda e, t: (e * steps + t, 0)),
-        ] + [VMEM_SPEC] * 5,
+        ] + [VMEM_SPEC],
         out_specs=[
             pl.BlockSpec((all_rows, tile), lambda e, t: (0, e * steps + t)),
             pl.BlockSpec((all_rows, tile), lambda e, t: (0, e * steps + t)),
@@ -742,20 +782,24 @@
             pltpu.VMEM((all_rows, width), BF16),
             pltpu.VMEM((own, width), F32),
             pltpu.VMEM((own, width), F32),
-            pltpu.VMEM((experts, wide * chunk, width), BF16),
-            pltpu.VMEM((experts, wide * chunk, width), BF16),
+            pltpu.VMEM((early, wide * chunk, width), BF16),
+            pltpu.VMEM((early, wide * chunk, width), BF16),
             pltpu.VMEM((plane, levels, share_rows, 4 * width), BF16),
             pltpu.VMEM((levels, share_rows, 4 * width), BF16),
             pltpu.VMEM((levels, share_rows, 4 * width), BF16),
-            dma((experts, wide)), dma((experts, wide)),
+            dma((early, wide)), dma((early, wide)),
             dma((plane,)), dma((plane,)), dma((levels,)), dma((levels,)),
         ],
-        compiler_params=remote_params(1),
+        compiler_params=remote_params(1, 56),
         name="regions",
     )(
         gathered, w_expert_in, b_expert_in[None, :], w_expert_out,
-        mine.reshape(levels, plane, share_rows, 4 * width), col, row, out_base, back_base,
-    )
+        mine.reshape(levels, plane, share_rows, 4 * width),
+    )
+    late_rows = (experts - early) * chunk
+    ret_late = lax.all_to_all(
+        ret_late.reshape(wide * late_rows, width), "wide", split_axis=0, concat_axis=0, tiled=True
+    ).reshape(wide, experts - early, chunk, width)
 
     half = width // narrow
     side = lax.axis_index("narrow")
@@ -784,8 +828,16 @@
             scratch_shapes=[pltpu.VMEM((half, all_rows), BF16), pltpu.VMEM((all_rows, half), BF16)],
         ),
         name="weights",
-        **params(8 * all_rows * half * slab, 8 * width * slab),
+        **params(8 * all_rows * half * slab, 8 * width * slab, 56),
     )(side.astype(jnp.int32)[None], gathered, hidden, grad_pre)
+    layer_out, grad_feats = pl.pallas_call(
+        functools.partial(sum_kernel, block_len, experts),
+        out_shape=(wide_bf, wide_bf),
+        in_specs=[VMEM_SPEC] * 6,
+        out_specs=[VMEM_SPEC] * 2,
+        name="sum",
+        **params(8 * points * all_rows * width, 8 * all_rows * width, 24),
+    )(col, row, ret_first, ret_late, out_base, back_base)
     bias_half = slab // narrow
     grad_bias_out = lax.dynamic_slice_in_dim(grad_bias[0], side * bias_half, bias_half, 0)
     return (layer_out, grad_feats, grad_attention, grad_in, grad_out_w, grad_bias_out)

time: 120 us -> 116 us (0.967)
  local copies, waits for them, and re-layouts: 10.3 us -> 4.16 us
  starting transfers between devices: 0 us -> 3.75 us
  Pallas kernels: 108 us -> 105 us
    pallas_call x1, Pallas kernels: 54.6 us -> 42.8 us  [on_device(): pl.pallas_call(functools.partial(region_kernel, (wide, plane, experts, bl...]
    unnamed x17 -> x13, local copies, waits for them, and re-layouts: 8.75 us -> 0.68 us
    pallas_call x1, Pallas kernels: 42 us -> 48.6 us  [on_device(): pl.pallas_call(functools.partial(attend_kernel, (wide, narrow, experts, b...]
    all_to_all x0 -> x1, starting transfers between devices: none -> 3.75 us  [on_device(): lax.all_to_all(ret_late.reshape(wide * late_rows, width), 'wide', split_a...]
    pallas_call x0 -> x1, Pallas kernels: none -> 1.59 us  [on_device(): pl.pallas_call(functools.partial(sum_kernel, block_len, experts), out_sha...]
    another operation x2, local copies, waits for them, and re-layouts: 0.19 us -> 1.42 us  [on_device(): col, row = (labels[:, None], labels[None, :])]
  transfers between devices with their start and end apart: 0 -> 1, of which waited for: 0 -> 1; matrix products, arithmetic and copies ran while one was open for 0% -> 1% of each run, Pallas kernels for 0% -> 11%
where the time goes in v3:
time: 116 us; the launch traced here: 115 us
  Pallas kernels  105 us (91%)
  local copies, waits for them, and re-layouts  4.16 us (4%)
  starting transfers between devices  3.75 us (3%)
    pallas_call x1, Pallas kernels, on_device(): pl.pallas_call(functools.partial(attend_kernel, (wide, narrow, experts, b...  48.6 us
    pallas_call x1, Pallas kernels, on_device(): pl.pallas_call(functools.partial(region_kernel, (wide, plane, experts, bl...  42.8 us
    pallas_call x1, Pallas kernels, on_device(): pl.pallas_call(functools.partial(weight_kernel, DOMAIN_SPECIALS / total,...  12.4 us
    all_to_all x1, starting transfers between devices, on_device(): lax.all_to_all(ret_late.reshape(wide * late_rows, width), 'wide', split_a...  3.75 us
  transfers between devices with their start and end apart: 1, of which 1 were waited for; matrix products, arithmetic and copies ran while one was open for 1% of the time, Pallas kernels for 11%

profile of v3, /device:TPU:0, one launch (start us, length us, event | category | flops | bytes accessed | tf_op | source)
XLA Modules:
  0.0 114.9 jit_solution(1396218288025559721)
XLA Ops:
  0.6 0.7 broadcast_in_dim.9
  1.4 0.8 broadcast_in_dim_reshape.8.col_ref
  2.1 0.7 broadcast_in_dim_reshape.7.row_ref
  2.8 48.6 %attend.1 = (bf16[512,2048]{1,0:T(8,128)(2,1)}, bf16[16,16,2048]{2,1,0:T(8,128)(2,1)}, f32[256,512]{1,0:T(8,128)}, f32[256,512]{1,0:T(8,128)}) custom-call(s32[256,1]{1,0:T(8,128)} %broadcast_in_dim_reshape.8.col_ref, s32[1,256]{1,0:T(1,128)} %broadcast_in_dim_reshape.7.row_ref, bf16[256,512]{1,0:T(8,128)(2,1)} %x_hbm.1, bf16[256,512]{1,0:T(8,128)(2,1)} %cot_hbm.1, ...), custom_call_target="tpu_custom_call" | custom-call | tf_op jit(solution)/shard_map/attend/pallas_call | solution.py:726
  51.4 42.8 %regions.1 = (bf16[256,8192]{1,0:T(8,128)(2,1)}, bf16[256,8192]{1,0:T(8,128)(2,1)}, bf16[2,256,512]{2,1,0:T(8,128)(2,1)}, bf16[16,2,16,512]{3,2,1,0:T(8,128)(2,1)}, f32[16,2048]{1,0:T(8,128)}) custom-call(bf16[512,2048]{1,0:T(8,128)(2,1)} %get-tuple-element.20.gath_ref.gath_feat_ref, bf16[512,8192]{1,0:T(8,128)(2,1)} %win_ref.1, f32[1,8192]{1,0:T(1,128)} %bitcast.9, ...), custom_call_target="tpu_custom_call" | custom-call | tf_op jit(solution)/shard_map/regions/pallas_call | solution.py:761
  94.2 0.0 copy-start
  94.2 0.0 copy-start.1
  94.2 0.0 copy-start.2
  94.2 0.0 copy-start.3
  94.2 0.0 copy-start.4
  94.2 3.8 %all-to-all-start = ((bf16[16,32,512]{2,1,0:T(8,128)(2,1)}), bf16[16,32,512]{2,1,0:T(8,128)(2,1)S(1)}, u32[]{:S(2)}, u32[]{:S(2)}) async-start(bf16[16,32,512]{2,1,0:T(8,128)(2,1)} %bitcast.8), calls=%async_computation | async-start | bytes 1048576 | tf_op jit(solution)/shard_map/all_to_all | solution.py:800
  98.0 0.0 copy-start.5
  98.0 12.4 %weights.1 = (f32[256,8192]{1,0:T(8,128)}, f32[8192,256]{1,0:T(8,128)}, f32[1,8192]{1,0:T(1,128)}) custom-call(s32[1]{0:T(128)} %bitcast.4.half_ref, bf16[512,2048]{1,0:T(8,128)(2,1)} %get-tuple-element.20.gath_ref.gath_feat_ref, bf16[256,8192]{1,0:T(8,128)(2,1)} %get-tuple-element.29.hidden_ref, bf16[256,8192]{1,0:T(8,128)(2,1)} %get-tuple-element.30.gpre_ref), custom_call_target="tpu_custom_call" | custom-call | flops 4294967296 | bytes 33554432 | tf_op jit(solution)/shard_map/weights/pallas_call | solution.py:808
  110.4 1.3 %constant_dynamic-slice_fusion = f32[1,4096]{1,0:T(1,128)} fusion(f32[1,8192]{1,0:T(1,128)} %get-tuple-element.33, s32[]{:T(128)S(6)} %select_n.3), kind=kLoop, calls=%fused_computation | loop fusion | bytes 32772 | tf_op jit(solution)/shard_map/dynamic_slice | solution.py:842
  111.7 0.9 all-to-all-done
  112.7 0.0 copy-done
  112.7 0.0 copy-done.1
  112.7 0.0 copy-done.2
  112.7 0.0 copy-done.3
  112.7 0.0 copy-done.4
  112.7 1.6 %sum.1 = (bf16[256,512]{1,0:T(8,128)(2,1)}, bf16[256,512]{1,0:T(8,128)(2,1)}) custom-call(s32[256,1]{1,0:T(8,128)S(1)} %copy-done, s32[1,256]{1,0:T(1,128)S(1)} %copy-done.4, bf16[2,256,512]{2,1,0:T(8,128)(2,1)S(1)} %copy-done.3, bf16[16,2,16,512]{3,2,1,0:T(8,128)(2,1)S(1)} %bitcast.6, f32[256,512]{1,0:T(8,128)S(1)} %copy-done.1, f32[256,512]{1,0:T(8,128)S(1)} %copy-done.2), custom_call_target="tpu_custom_call" | custom-call | flops 268435456 | bytes 1048576 | tf_op jit(solution)/shard_map/sum/pallas_call | solution.py:833
  114.3 0.0 copy-done.5
  114.3 0.7 copy.17
Async XLA Ops:
  94.2 18.5 %copy-start = (s32[256,1]{1,0:T(8,128)S(1)}, s32[256,1]{1,0:T(8,128)}, u32[]{:S(2)}) copy-start(s32[256,1]{1,0:T(8,128)} %broadcast_in_dim_reshape.8.col_ref) | copy-start | bytes 3076
  94.2 18.5 %copy-start.1 = (f32[256,512]{1,0:T(8,128)S(1)}, f32[256,512]{1,0:T(8,128)}, u32[]{:S(2)}) copy-start(f32[256,512]{1,0:T(8,128)} %get-tuple-element.24.out_base_ref) | copy-start | bytes 1572868
  94.2 18.5 %copy-start.2 = (f32[256,512]{1,0:T(8,128)S(1)}, f32[256,512]{1,0:T(8,128)}, u32[]{:S(2)}) copy-start(f32[256,512]{1,0:T(8,128)} %get-tuple-element.25.back_base_ref) | copy-start | bytes 1572868
  94.2 18.5 %copy-start.3 = (bf16[2,256,512]{2,1,0:T(8,128)(2,1)S(1)}, bf16[2,256,512]{2,1,0:T(8,128)(2,1)}, u32[]{:S(2)}) copy-start(bf16[2,256,512]{2,1,0:T(8,128)(2,1)} %get-tuple-element.22.first_ref) | copy-start | bytes 1572868
  94.2 18.5 %copy-start.4 = (s32[1,256]{1,0:T(1,128)S(1)}, s32[1,256]{1,0:T(1,128)}, u32[]{:S(2)}) copy-start(s32[1,256]{1,0:T(1,128)} %broadcast_in_dim_reshape.7.row_ref) | copy-start | bytes 3076
  94.2 18.4 %all-to-all-start = ((bf16[16,32,512]{2,1,0:T(8,128)(2,1)}), bf16[16,32,512]{2,1,0:T(8,128)(2,1)S(1)}, u32[]{:S(2)}, u32[]{:S(2)}) async-start(bf16[16,32,512]{2,1,0:T(8,128)(2,1)} %bitcast.8), calls=%async_computation | async-start | bytes 1048576 | tf_op jit(solution)/shard_map/all_to_all | solution.py:800
  98.0 16.3 %copy-start.5 = (f32[16,2048]{1,0:T(8,128)S(1)}, f32[16,2048]{1,0:T(8,128)}, u32[]{:S(2)}) copy-start(f32[16,2048]{1,0:T(8,128)} %get-tuple-element.42) | copy-start | bytes 393220
